TPU v7x, 128 devices: a whole 4x4x4 slice. The times are simulated.
128 devices in a mesh: depth: 16 (over y, x), cross: 8 (over z, core).
Axes of the slice: x: 4, y: 4, z: 4, core: 2. Of those that a mesh axis runs over, the one named last changes fastest.
Arguments:
- flame_heat_values: bfloat16 [256, 1024, 2048], P('depth', 'cross'), may hold values from -6 to 6
- lookup_entry_index: int32 [256, 1024, 2048], P('depth', 'cross'), may hold values from 0 to 15
- transfer_lookup_table: float32 [4, 16], replicated, may hold values from 0.1 to 1
Outputs:
- picture: float32 [4, 1024, 2048], P(None, 'cross', 'depth')
All inputs are finite; a program needn't handle non-finite values.
Results may differ from a plain program's by a relative error of at most 0.0003.
Values may be sent and summed in bfloat16 or wider, within the bound.
No kernel may reach another device: no remote copies, remote signals or barrier semaphores. Data moves between devices by JAX's collectives and lax.ppermute only.
A program may use at most 320 MiB of HBM per device.

v0:
```python
import jax
import jax.numpy as jnp
from jax import lax
from jax.sharding import PartitionSpec as P


def padded(block, sides, width):
    for axis, dim in sides:
        count = lax.axis_size(axis)
        forward = [(i, i + 1) for i in range(count - 1)]
        backward = [(target, source) for source, target in forward]
        low = lax.ppermute(
            lax.slice_in_dim(block, block.shape[dim] - width, None, axis=dim), axis, forward
        )
        high = lax.ppermute(lax.slice_in_dim(block, 0, width, axis=dim), axis, backward)
        block = jnp.concatenate([low, block, high], axis=dim)
    return block


def swapped(value, axis, apart):
    mask = 2**apart
    pairs = [(source, source ^ mask) for source in range(lax.axis_size(axis))]
    return lax.ppermute(value, axis, pairs)


def blend(front, back):
    return jnp.concatenate([front[:3] + front[3:] * back[:3], front[3:] * back[3:]], axis=0)


def local(flame_heat_values, lookup_entry_index, transfer_lookup_table):
    haloed_heat_mesh = padded(flame_heat_values, (("depth", 0), ("cross", 1)), 1)
    accelerator_array = lax.axis_size("depth")
    entire_sight_extent = flame_heat_values.shape[0] * accelerator_array
    scale_alpha = 4.0 / entire_sight_extent
    rows = flame_heat_values.shape[1]
    columns = flame_heat_values.shape[2]
    entries = transfer_lookup_table.shape[1]
    heat_block = jnp.pad(haloed_heat_mesh.astype(jnp.float32), ((0, 0), (0, 0), (1, 1)))
    centre = heat_block[1:-1, 1:-1, 1:-1]
    grad_depth = 0.5 * (heat_block[2:, 1:-1, 1:-1] - heat_block[:-2, 1:-1, 1:-1])
    grad_row = 0.5 * (heat_block[1:-1, 2:, 1:-1] - heat_block[1:-1, :-2, 1:-1])
    grad_col = 0.5 * (heat_block[1:-1, 1:-1, 2:] - heat_block[1:-1, 1:-1, :-2])
    lit = grad_depth * (1.0 / 3.0) + grad_row * (2.0 / 3.0) + grad_col * (2.0 / 3.0)
    square = grad_depth * grad_depth + grad_row * grad_row + grad_col * grad_col
    shade = 0.3 + 0.7 * lit * lit / (square + 1.0)
    looked = [jnp.zeros(centre.shape, jnp.float32) for channel in range(4)]
    for number in range(entries):
        matched = lookup_entry_index == number
        looked = [
            jnp.where(matched, transfer_lookup_table[channel, number], looked[channel])
            for channel in range(4)
        ]
    alpha = scale_alpha * looked[3] * jax.nn.sigmoid(2.0 * centre)
    through = jnp.cumprod(1.0 - alpha, axis=0)
    before = jnp.concatenate([jnp.ones((1, rows, columns), jnp.float32), through[:-1]], axis=0)
    weight = shade * alpha * before
    colors = jnp.stack([jnp.sum(looked[channel] * weight, axis=0) for channel in range(3)], axis=0)
    trans = through[-1]
    image = jnp.concatenate([colors, trans[None]], axis=0)
    width = columns // accelerator_array
    level_count = accelerator_array.bit_length() - 1
    blocks = image.reshape((4, rows) + (2,) * level_count + (width,))
    order = (0, 1) + tuple(range(level_count + 1, 1, -1)) + (level_count + 2,)
    current = jnp.transpose(blocks, order).reshape(4, rows, accelerator_array * width)
    position = lax.axis_index("depth")
    for level in range(level_count):
        half = current.shape[2] // 2
        lower = current[:, :, :half]
        upper = current[:, :, half:]
        upper_side = position >> level & 1 == 1
        kept = jnp.where(upper_side, upper, lower)
        sent = jnp.where(upper_side, lower, upper)
        received = swapped(sent, "depth", level)
        front = jnp.where(upper_side, received, kept)
        back = jnp.where(upper_side, kept, received)
        current = blend(front, back)
    return jnp.concatenate([current[:3], 1.0 - current[3:]], axis=0)


def solution(mesh):
    in_specs = (P("depth", "cross", None), P("depth", "cross", None), P())
    out_specs = P(None, "cross", "depth")
    return jax.shard_map(local, mesh=mesh, in_specs=in_specs, out_specs=out_specs, check_vma=False)
```

profile of v0, /device:TPU:0, one launch (start us, length us, event | category | flops | bytes accessed | tf_op | source)
XLA Modules:
  0.0 437.4 jit_solution(3030155907479724440)
XLA Ops:
  1.3 3.5 collective-permute-start
  12.4 3.5 collective-permute-done
  16.8 8.3 %constant_dynamic-update-slice_fusion.1 = bf16[18,128,2048]{2,1,0:T(8,128)(2,1)} fusion(bf16[18,128,2048]{2,1,0:T(8,128)(2,1)} %constant_dynamic-update-slice_fusion.2, bf16[16,128,2048]{2,1,0:T(8,128)(2,1)} %param.3), kind=kLoop, calls=%fused_computation.87 | loop fusion | bytes 16777216
  28.7 3.0 collective-permute-start.2
  32.8 13.7 %maximum_convert_fusion = f32[18,130,2048]{2,1,0:T(8,128)} fusion(bf16[18,1,2048]{2,1,0:T(2,128)(2,1)S(1)} %collective-permute-done.3, bf16[18,128,2048]{2,1,0:T(8,128)(2,1)} %constant_dynamic-update-slice_fusion, bf16[18,1,2048]{2,1,0:T(2,128)(2,1)S(1)} %collective-permute-done.2), kind=kLoop, calls=%fused_computation.21 | loop fusion | flops 28753920 | bytes 28753920 | tf_op jit(solution)/shard_map/convert_element_type | solution.py:38
  46.4 72.7 %fusion.9 = (f32[16,128,2048]{2,1,0:T(8,128)}, pred[16,128,2048]{2,1,0:T(8,128)(4,1)}, pred[16,128,2048]{2,1,0:T(8,128)(4,1)}, pred[16,128,2048]{2,1,0:T(8,128)(...) fusion(f32[18,130,2048]{2,1,0:T(8,128)} %maximum_convert_fusion, ...), kind=kLoop, calls=%fused_computation.13 | loop fusion | flops 159383552 | bytes 117440576 | tf_op jit(solution)/shard_map/mul | solution.py:53
  119.1 12.4 %fusion.10 = f32[16,128,2048]{2,1,0:T(8,128)} fusion(f32[16,128,2048]{2,1,0:T(8,128)} %get-tuple-element.7), kind=kOutput, calls=%fused_computation.19 | output fusion | flops 67108864 | bytes 33554432 | tf_op jit(solution)/shard_map/jit(cumprod)/reduce_window | solution.py:54
  131.5 14.0 %slice.420 = f32[15,128,2048]{2,1,0:T(8,128)} slice(f32[16,128,2048]{2,1,0:T(8,128)} %fusion.10), slice={[0:15], [0:128], [0:2048]} | slice | bytes 31457280 | tf_op jit(solution)/shard_map/slice | solution.py:55
  146.4 78.8 %multiply_reduce_fusion.2 = (f32[128,2048]{1,0:T(8,128)S(1)}, f32[16,128,2048]{2,1,0:T(8,128)}) fusion(pred[16,128,2048]{2,1,0:T(8,128)(4,1)} %get-tuple-element.23, pred[16,128,2048]{2,1,0:T(8,128)(4,1)} %get-tuple-element.22, pred[16,128,2048]{2,1,0:T(8,128)(4,1)} %get-tuple-element.21, pred[16,128,2048]{2,1,0:T(8,128)(4,1)} %get-tuple-element.20, ...), kind=kLoop, calls=%fused_computation.18 | loop fusion | flops 171704320 | bytes 204611584 | tf_op jit(solution)/shard_map/reduce_sum | solution.py:57
  225.2 41.1 %multiply_reduce_fusion = f32[128,2048]{1,0:T(8,128)S(1)} fusion(f32[16,128,2048]{2,1,0:T(8,128)} %get-tuple-element.6, pred[16,128,2048]{2,1,0:T(8,128)(4,1)} %get-tuple-element.23, pred[16,128,2048]{2,1,0:T(8,128)(4,1)} %get-tuple-element.22, pred[16,128,2048]{2,1,0:T(8,128)(4,1)} %get-tuple-element.21, pred[16,128,2048]{2,1,0:T(8,128)(4,1)} %get-tuple-element.20, ...), kind=kLoop, calls=%fused_computation.16 | loop fusion | flops 75235328 | bytes 84934720 | tf_op jit(solution)/shard_map/reduce_sum | solution.py:57
  268.2 41.4 %multiply_reduce_fusion.1 = f32[128,2048]{1,0:T(8,128)S(1)} fusion(f32[16,128,2048]{2,1,0:T(8,128)} %get-tuple-element.6, pred[16,128,2048]{2,1,0:T(8,128)(4,1)} %get-tuple-element.23, pred[16,128,2048]{2,1,0:T(8,128)(4,1)} %get-tuple-element.22, pred[16,128,2048]{2,1,0:T(8,128)(4,1)} %get-tuple-element.21, pred[16,128,2048]{2,1,0:T(8,128)(4,1)} %get-tuple-element.20, ...), kind=kLoop, calls=%fused_computation.17 | loop fusion | flops 75235328 | bytes 84934720 | tf_op jit(solution)/shard_map/reduce_sum | solution.py:57
  312.4 3.6 maximum_bitcast_fusion
  316.0 4.1 copy.4
  320.1 6.4 %reshape.11 = f32[4,128,2048]{2,1,0:T(8,128)} reshape(f32[4,128,2,2,2,2,128]{6,5,4,3,2,1,0:T(2,128)} %copy.4) | data formatting | bytes 8388608 | tf_op jit(solution)/shard_map/reshape | solution.py:64
  326.5 2.6 slice_select_fusion.1
  329.1 2.6 collective-permute-start.4
  331.7 44.6 %collective-permute-done.4 = f32[4,128,1024]{2,1,0:T(8,128)} collective-permute-done((f32[4,128,1024]{2,1,0:T(8,128)S(1)}, f32[4,128,1024]{2,1,0:T(8,128)}, u32[]{:S(2)}, u32[]{:S(2)}) %collective-permute-start.4) | collective-permute-done | bytes 2097184 | tf_op jit(solution)/shard_map/ppermute | solution.py:23
  376.3 3.6 broadcast_select_fusion.1
  380.5 3.9 collective-permute-start.5
  384.5 23.3 %collective-permute-done.5 = f32[4,128,512]{2,1,0:T(8,128)} collective-permute-done((f32[4,128,512]{2,1,0:T(8,128)S(1)}, f32[4,128,512]{2,1,0:T(8,128)}, u32[]{:S(2)}, u32[]{:S(2)}) %collective-permute-start.5) | collective-permute-done | bytes 1048608 | tf_op jit(solution)/shard_map/ppermute | solution.py:23
  409.6 4.6 %collective-permute-start.6 = (f32[4,128,256]{2,1,0:T(8,128)S(1)}, f32[4,128,256]{2,1,0:T(8,128)S(1)}, u32[]{:S(2)}, u32[]{:S(2)}) collective-permute-start(f32[4,128,256]{2,1,0:T(8,128)S(1)} %broadcast_select_fusion.9), channel_id=1, source_target_pairs={{0,32},{8,40},{16,48},{24,56},{32,0},{40,8},{48,16},{56,24},{64,96... | collective-permute-start | bytes 1572872 | tf_op jit(solution)/shard_map/ppermute | solution.py:23
  414.2 12.4 %collective-permute-done.6 = f32[4,128,256]{2,1,0:T(8,128)S(1)} collective-permute-done((f32[4,128,256]{2,1,0:T(8,128)S(1)}, f32[4,128,256]{2,1,0:T(8,128)S(1)}, u32[]{:S(2)}, u32[]{:S(2)}) %collective-permute-start.6) | collective-permute-done | bytes 524320 | tf_op jit(solution)/shard_map/ppermute | solution.py:23
  426.9 3.4 collective-permute-start.7
  430.3 6.2 %collective-permute-done.7 = f32[4,128,128]{2,1,0:T(8,128)S(1)} collective-permute-done((f32[4,128,128]{2,1,0:T(8,128)S(1)}, f32[4,128,128]{2,1,0:T(8,128)S(1)}, u32[]{:S(2)}, u32[]{:S(2)}) %collective-permute-start.7) | collective-permute-done | bytes 262176 | tf_op jit(solution)/shard_map/ppermute | solution.py:23
  (36 shorter events, 23.4 us)
Async XLA Ops:
  0.0 31.8 %copy-start = (f32[4,16]{1,0:T(4,128)S(1)}, f32[4,16]{1,0:T(4,128)}, u32[]{:S(2)}) copy-start(f32[4,16]{1,0:T(4,128)} %param.5) | copy-start | bytes 772
  1.3 14.7 %collective-permute-start = (bf16[1,128,2048]{2,1,0:T(8,128)(2,1)S(1)}, bf16[1,128,2048]{2,1,0:T(8,128)(2,1)S(1)}, u32[]{:S(2)}, u32[]{:S(2)}) collective-permute-start(bf16[1,128,2048]{2,1,0:T(8,128)(2,1)S(1)} %get-tuple-element.27), channel_id=1, source_target_pairs={{0,8},{8,16},{16,24},{24,32},{32,40},{40,48},{48,56},{56,64},{64,7... | collective-permute-start | bytes 1572872 | tf_op jit(solution)/shard_map/ppermute | solution.py:12
  4.8 20.3 %collective-permute-start.1 = (bf16[1,128,2048]{2,1,0:T(8,128)(2,1)S(1)}, bf16[1,128,2048]{2,1,0:T(8,128)(2,1)S(1)}, u32[]{:S(2)}, u32[]{:S(2)}) collective-permute-start(bf16[1,128,2048]{2,1,0:T(8,128)(2,1)S(1)} %get-tuple-element.26), channel_id=1, source_target_pairs={{8,0},{16,8},{24,16},{32,24},{40,32},{48,40},{56,48},{64,56},{72,6... | collective-permute-start | bytes 1572872 | tf_op jit(solution)/shard_map/ppermute | solution.py:15
  27.4 5.0 %collective-permute-start.3 = (bf16[18,1,2048]{2,1,0:T(2,128)(2,1)S(1)}, bf16[18,1,2048]{2,1,0:T(2,128)(2,1)S(1)}, u32[]{:S(2)}, u32[]{:S(2)}) collective-permute-start(bf16[18,1,2048]{2,1,0:T(2,128)(2,1)S(1)} %get-tuple-element.25), channel_id=1, source_target_pairs={{1,0},{2,1},{3,2},{4,3},{5,4},{6,5},{7,6},{9,8},{10,9},{11,10},{12... | collective-permute-start | bytes 221192 | tf_op jit(solution)/shard_map/ppermute | solution.py:15
  28.7 4.0 collective-permute-start.2
  131.5 14.0 %slice-start = ((f32[16,128,2048]{2,1,0:T(8,128)}), f32[1,128,2048]{2,1,0:T(8,128)S(1)}, s32[]{:S(2)}) async-start(f32[16,128,2048]{2,1,0:T(8,128)} %fusion.10), calls=%async_computation | async-start | bytes 2097152 | tf_op jit(solution)/shard_map/slice | solution.py:58
  329.1 47.1 %collective-permute-start.4 = (f32[4,128,1024]{2,1,0:T(8,128)S(1)}, f32[4,128,1024]{2,1,0:T(8,128)}, u32[]{:S(2)}, u32[]{:S(2)}) collective-permute-start(f32[4,128,1024]{2,1,0:T(8,128)S(1)} %slice_select_fusion.1), channel_id=1, source_target_pairs={{0,8},{8,0},{16,24},{24,16},{32,40},{40,32},{48,56},{56,48},{64,72... | collective-permute-start | bytes 6291464 | tf_op jit(solution)/shard_map/ppermute | solution.py:23
  380.5 27.2 %collective-permute-start.5 = (f32[4,128,512]{2,1,0:T(8,128)S(1)}, f32[4,128,512]{2,1,0:T(8,128)}, u32[]{:S(2)}, u32[]{:S(2)}) collective-permute-start(f32[4,128,512]{2,1,0:T(8,128)S(1)} %broadcast_select_fusion.5), channel_id=1, source_target_pairs={{0,16},{8,24},{16,0},{24,8},{32,48},{40,56},{48,32},{56,40},{64,80... | collective-permute-start | bytes 3145736 | tf_op jit(solution)/shard_map/ppermute | solution.py:23
  409.6 17.0 %collective-permute-start.6 = (f32[4,128,256]{2,1,0:T(8,128)S(1)}, f32[4,128,256]{2,1,0:T(8,128)S(1)}, u32[]{:S(2)}, u32[]{:S(2)}) collective-permute-start(f32[4,128,256]{2,1,0:T(8,128)S(1)} %broadcast_select_fusion.9), channel_id=1, source_target_pairs={{0,32},{8,40},{16,48},{24,56},{32,0},{40,8},{48,16},{56,24},{64,96... | collective-permute-start | bytes 1572872 | tf_op jit(solution)/shard_map/ppermute | solution.py:23
  426.9 9.7 %collective-permute-start.7 = (f32[4,128,128]{2,1,0:T(8,128)S(1)}, f32[4,128,128]{2,1,0:T(8,128)S(1)}, u32[]{:S(2)}, u32[]{:S(2)}) collective-permute-start(f32[4,128,128]{2,1,0:T(8,128)S(1)} %broadcast_select_fusion.13), channel_id=1, source_target_pairs={{0,64},{8,72},{16,80},{24,88},{32,96},{40,104},{48,112},{56,120},{... | collective-permute-start | bytes 786440 | tf_op jit(solution)/shard_map/ppermute | solution.py:23
where the time goes:
time: 439 us; the launch traced here: 437 us
  other arithmetic  273 us (62%)
  waiting for transfers between devices  90.3 us (21%)
  local copies, waits for them, and re-layouts  49.8 us (11%)
  starting transfers between devices  23.6 us (5%)
    reduce_sum x3, other arithmetic, local(): jnp.sum(looked[channel] * weight, axis=0)  161 us
    ppermute x4, waiting for transfers between devices, swapped(): return lax.ppermute(value, axis, pairs)  86.5 us
    mul x1, other arithmetic, local(): alpha = scale_alpha * looked[3] * jax.nn.sigmoid(2.0 * centre)  72.7 us
    ppermute x4, starting transfers between devices, swapped(): return lax.ppermute(value, axis, pairs)  14.5 us
    slice x1, local copies, waits for them, and re-layouts, local(): through[:-1]  14 us
    convert_element_type x1, other arithmetic, local(): haloed_heat_mesh.astype(jnp.float32)  13.7 us
    another operation x1, other arithmetic, local(): through = jnp.cumprod(1.0 - alpha, axis=0)  12.4 us
    unnamed x4, local copies, waits for them, and re-layouts  9.15 us
  transfers between devices with their start and end apart: 8, of which 6 were waited for; matrix products, arithmetic and copies ran while one was open for 4% of the time, Pallas kernels for 0%

commit v1 on v0

v1 whole, which is shorter than its diff:
```python
import functools

import jax
import jax.numpy as jnp
import numpy as np
from jax import lax
from jax.experimental import pallas as pl
from jax.experimental.pallas import tpu as pltpu
from jax.sharding import PartitionSpec as P

LANES = 128
SUBLANES = 8
PARTS = 2
UNITS = 4
WIDTH = 1024
PIECES = 16
f32 = jnp.float32
LANE_LOOKUP = lax.GatherDimensionNumbers(
    offset_dims=(),
    collapsed_slice_dims=(1,),
    start_index_map=(1,),
    operand_batching_dims=(0,),
    start_indices_batching_dims=(0,),
)
KAPPA = -2.0 / float(np.log(2.0))
HIGH_STEPS = 32766.0
LOW_STEPS = 65535.0
CENTRE = 16.0
STEPS = 2340.0
LEAST = 2.0**-29.9


def brick_kernel(table_ref, diff_ref, left_ref, heat_ref, right_ref, above_ref, below_ref, before_ref, after_ref, upper_ref,
                 lower_ref, entry_ref, out_ref, t, dv, *, block, blocks, sight):
    layers, rows, width = heat_ref.shape
    strips = width // LANES
    j = pl.program_id(0)
    opaque = LOW_STEPS * sight / 4.0
    bias = float(np.log2(opaque))

    def kept(value):
        return value.astype(f32) * KAPPA + bias

    for s in range(strips):
        cols = slice(s * LANES, (s + 1) * LANES)

        def convert(z, carry):
            t[z + 1, s, 0:8, :] = kept(above_ref[z, 8:16, cols])
            t[z + 1, s, 8 : 8 + rows, :] = kept(heat_ref[z, :, cols])
            t[z + 1, s, 8 + rows : 16 + rows, :] = kept(below_ref[z, 0:8, cols])
            return carry

        lax.fori_loop(0, layers, convert, 0, unroll=4)
        t[0, s, 8 : 8 + rows, :] = kept(before_ref[:, cols])
        t[layers + 1, s, 8 : 8 + rows, :] = kept(after_ref[:, cols])
        if block == 0:
            up = kept(upper_ref[:, cols])
            for z in range(layers):
                t[z + 1, s, 7:8, :] = up[z : z + 1]
        if block == blocks - 1:
            low = kept(lower_ref[:, cols])
            for z in range(layers):
                t[z + 1, s, 8 + rows : 9 + rows, :] = low[z : z + 1]

    zero = jnp.zeros((), jnp.bfloat16)
    left = jnp.where(j == 0, zero, left_ref[...])
    right = jnp.where(j == pl.num_programs(0) - 1, zero, right_ref[...])
    pieces = [left] + [heat_ref[:, :, s * LANES : (s + 1) * LANES] for s in range(strips)] + [right]
    for s in range(0, strips, 2):
        window = jnp.concatenate(pieces[s : s + 4], axis=2).reshape(layers * rows, 4 * LANES)
        moved = jnp.dot(window, diff_ref[...], preferred_element_type=f32).reshape(layers, rows, 2 * LANES)
        dv[:, s] = moved[:, :, :LANES] * KAPPA
        dv[:, s + 1] = moved[:, :, LANES:] * KAPPA

    tables = [jnp.broadcast_to(table_ref[pair : pair + 1, :], (SUBLANES, LANES)) for pair in range(2)]

    def looked(entry):
        rg, ba = [
            lax.gather(table, entry[:, :, None], LANE_LOOKUP, (1, 1), mode=lax.GatherScatterMode.PROMISE_IN_BOUNDS)
            for table in tables
        ]
        return rg.astype(f32), (rg & 0xFFFF).astype(f32), ba.astype(f32), (ba & 0xFFFF).astype(f32)

    scale = 0.7 / 9.0
    scales = [scale / (HIGH_STEPS * 65536.0), scale / LOW_STEPS, scale / (HIGH_STEPS * 65536.0)]
    groups = rows // (SUBLANES * UNITS)

    def body(g, carry):
        s = g // groups
        cols = pl.ds(pl.multiple_of(s * LANES, LANES), LANES)
        units = []
        for u in range(UNITS):
            r0 = pl.multiple_of((g % groups) * (SUBLANES * UNITS) + u * SUBLANES, SUBLANES)
            units.append(
                dict(
                    r0=r0,
                    trans=jnp.ones((SUBLANES, LANES), f32),
                    colors=[jnp.zeros((SUBLANES, LANES), f32) for channel in range(3)],
                    prev=t[0, s, pl.ds(8 + r0, 8), :],
                    cur=t[1, s, pl.ds(8 + r0, 8), :],
                )
            )
        for z in range(layers):
            for unit in units:
                r0 = unit["r0"]
                nxt = t[z + 2, s, pl.ds(8 + r0, 8), :]
                a = nxt - unit["prev"]
                b = t[z + 1, s, pl.ds(9 + r0, 8), :] - t[z + 1, s, pl.ds(7 + r0, 8), :]
                c = dv[z, s, pl.ds(r0, 8), :]
                m = b + c
                lit = a + m + m
                square = (a * a + b * b) + (c * c + 4.0 * KAPPA * KAPPA)
                shade = lit * lit * pl.reciprocal(square, approx=True) + 0.3 / scale
                red, green, blue, weight = looked(entry_ref[z, pl.ds(r0, 8), cols])
                alpha = weight * pl.reciprocal(jnp.exp2(unit["cur"]) + opaque, approx=True)
                part = alpha * unit["trans"]
                unit["trans"] = unit["trans"] - part
                shown = shade * part
                unit["colors"] = [old + new * shown for old, new in zip(unit["colors"], (red, green, blue))]
                unit["prev"], unit["cur"] = unit["cur"], nxt
        for pair in range(0, UNITS, 2):
            both = units[pair : pair + 2]
            for channel in range(4):
                value = jnp.concatenate(
                    [unit["colors"][channel] * scales[channel] if channel < 3 else 1.0 - unit["trans"] for unit in both], axis=0
                )
                code = jnp.round((jnp.log2(jnp.maximum(value, LEAST)) + CENTRE) * STEPS)
                out_ref[s, channel, pl.ds(pl.multiple_of(both[0]["r0"], 16), 16), :] = code.astype(jnp.int32).astype(jnp.int16)
        return carry

    lax.fori_loop(0, strips * groups, body, 0)


def brick(table, diff, heat, before, after, upper, lower, entry, block, sight):
    layers, all_rows, columns = heat.shape
    rows = all_rows // PARTS
    n = columns // WIDTH
    per = WIDTH // LANES
    col_blocks = columns // LANES
    sub = rows // 16
    return pl.pallas_call(
        functools.partial(brick_kernel, block=block, blocks=PARTS, sight=sight),
        grid=(n,),
        in_specs=[
            pl.BlockSpec((2, LANES), lambda j: (0, 0)),
            pl.BlockSpec((4 * LANES, 2 * LANES), lambda j: (0, 0)),
            pl.BlockSpec((layers, rows, LANES), lambda j: (0, block, jnp.maximum(j * per - 1, 0))),
            pl.BlockSpec((layers, rows, WIDTH), lambda j: (0, block, j)),
            pl.BlockSpec((layers, rows, LANES), lambda j: (0, block, jnp.minimum(j * per + per, col_blocks - 1))),
            pl.BlockSpec((layers, 16, WIDTH), lambda j: (0, max(sub * block - 1, 0), j)),
            pl.BlockSpec((layers, 16, WIDTH), lambda j: (0, min(sub * block + sub, all_rows // 16 - 1), j)),
            pl.BlockSpec((rows, WIDTH), lambda j: (block, j)),
            pl.BlockSpec((rows, WIDTH), lambda j: (block, j)),
            pl.BlockSpec((layers, WIDTH), lambda j: (0, j)),
            pl.BlockSpec((layers, WIDTH), lambda j: (0, j)),
            pl.BlockSpec((layers, rows, WIDTH), lambda j: (0, block, j)),
        ],
        out_specs=pl.BlockSpec((per, 4, rows, LANES), lambda j: (j, 0, 0, 0)),
        out_shape=jax.ShapeDtypeStruct((col_blocks, 4, rows, LANES), jnp.int16),
        scratch_shapes=[
            pltpu.VMEM((layers + 2, per, rows + 16, LANES), f32),
            pltpu.VMEM((layers, per, rows, LANES), f32),
        ],
        compiler_params=pltpu.CompilerParams(vmem_limit_bytes=56 * 1024 * 1024),
        name="brick",
    )(table, diff, heat, heat, heat, heat, heat, before, after, upper, lower, entry)


def merge_kernel(got_ref, *rest):
    out_ref = rest[-1]
    count, channels, rows, lanes = got_ref.shape

    def body(g, carry):
        here = pl.ds(pl.multiple_of(g * 16, 16), 16)
        colors = [jnp.zeros((16, lanes), f32) for channel in range(3)]
        trans = jnp.ones((16, lanes), f32)
        for source in range(count):
            value = [
                jnp.exp2(got_ref[source, channel, here, :].astype(f32) * (1.0 / STEPS) - CENTRE) for channel in range(4)
            ]
            colors = [old + trans * new for old, new in zip(colors, value)]
            trans = trans - trans * value[3]
        for channel in range(4):
            out_ref[channel, here, :] = colors[channel] if channel < 3 else 1.0 - trans
        return carry

    lax.fori_loop(0, rows // 16, body, 0)


def merge(got, block, image):
    count, channels, rows, lanes = got.shape
    here = pl.BlockSpec((channels, rows, lanes), lambda i: (0, block, 0))
    operands, specs, aliases = [got], [pl.BlockSpec(got.shape, lambda i: (0, 0, 0, 0))], {}
    if image is not None:
        operands.append(image)
        specs.append(pl.BlockSpec(memory_space=pl.ANY))
        aliases = {1: 0}
    return pl.pallas_call(
        merge_kernel,
        grid=(1,),
        in_specs=specs,
        out_specs=here,
        out_shape=jax.ShapeDtypeStruct((channels, rows * PARTS, lanes), f32),
        input_output_aliases=aliases,
        name="merge",
    )(*operands)


def difference_matrix():
    m = np.zeros((4 * LANES, 2 * LANES), np.float32)
    n = np.arange(2 * LANES)
    m[LANES + n + 1, n] = 1
    m[LANES + n - 1, n] = -1
    return jnp.asarray(m, jnp.bfloat16)


def packed(table):
    low = jnp.round(table[1::2] * LOW_STEPS)
    high = jnp.round(table[0::2] * HIGH_STEPS - low * (1.0 / 65536.0))
    words = high.astype(jnp.int32) * 65536 + low.astype(jnp.int32)
    return jnp.pad(words, ((0, 0), (0, LANES - table.shape[1])))


def local(heat, entry, table):
    count = lax.axis_size("depth")
    sides = lax.axis_size("cross")
    sight = heat.shape[0] * count
    on, back = [(i, i + 1) for i in range(count - 1)], [(i + 1, i) for i in range(count - 1)]
    down, up = [(i, i + 1) for i in range(sides - 1)], [(i + 1, i) for i in range(sides - 1)]
    upper = lax.ppermute(heat[:, -1, :], "cross", down)
    lower = lax.ppermute(heat[:, 0, :], "cross", up)
    before = lax.ppermute(heat[-1], "depth", on)
    after = lax.ppermute(heat[0], "depth", back)
    words, diff = packed(table), difference_matrix()
    image = None
    sent = []
    for block in range(PARTS):
        codes = brick(words, diff, heat, before, after, upper, lower, entry, block, sight)
        sent.append(lax.all_to_all(codes, "depth", 0, 0, tiled=True))
    for block in range(PARTS):
        image = merge(sent[block], block, image)
    return image


def solution(mesh):
    in_specs = (P("depth", "cross", None), P("depth", "cross", None), P())
    out_specs = P(None, "cross", "depth")
    return jax.shard_map(local, mesh=mesh, in_specs=in_specs, out_specs=out_specs, check_vma=False)
```

time: 439 us -> 102 us (0.23)
  other arithmetic: 273 us -> 0.01 us
  waiting for transfers between devices: 90.3 us -> 19.3 us
  Pallas kernels: 0 us -> 50 us
  local copies, waits for them, and re-layouts: 49.8 us -> 6.56 us
    reduce_sum x3 -> x0, other arithmetic: 161 us -> none  [local(): jnp.sum(looked[channel] * weight, axis=0)]
    ppermute x8 -> x4, waiting for transfers between devices: 90.3 us -> 4.56 us  [the longest x1 2.06 us: local(): lower = lax.ppermute(heat[:, 0, :], 'cross', up)]
    mul x5 -> x0, other arithmetic: 72.8 us -> none  [the longest x1 72.7 us: local(): alpha = scale_alpha * looked[3] * jax.nn.sigmoid(2.0 * centre)]
    pallas_call x0 -> x4, Pallas kernels: none -> 50 us  [the longest x2 45.2 us: brick(): pl.pallas_call(functools.partial(brick_kernel, block=block, blocks=PARTS,...]
    slice x9 -> x3, local copies, waits for them, and re-layouts: 23.7 us -> 2.81 us  [the longest x1 1.41 us: local(): lower = lax.ppermute(heat[:, 0, :], 'cross', up)]
    all_to_all x0 -> x2, starting transfers between devices: none -> 17.4 us  [local(): sent.append(lax.all_to_all(codes, 'depth', 0, 0, tiled=True))]
    ppermute x8 -> x4, starting transfers between devices: 23.6 us -> 8.46 us  [the longest x1 4.58 us: local(): before = lax.ppermute(heat[-1], 'depth', on)]
    all_to_all x0 -> x2, waiting for transfers between devices: none -> 14.7 us  [local(): sent.append(lax.all_to_all(codes, 'depth', 0, 0, tiled=True))]
  transfers between devices with their start and end apart: 8 -> 6, of which waited for: 6 -> 4; matrix products, arithmetic and copies ran while one was open for 4% -> 3% of each run, Pallas kernels for 0% -> 25%
where the time goes in v1:
time: 102 us
  Pallas kernels  50 us (49%)
  starting transfers between devices  25.8 us (25%)
  waiting for transfers between devices  19.3 us (19%)
  local copies, waits for them, and re-layouts  6.56 us (6%)
    pallas_call x2, Pallas kernels, brick(): pl.pallas_call(functools.partial(brick_kernel, block=block, blocks=PARTS,...  45.2 us
    all_to_all x2, starting transfers between devices, local(): sent.append(lax.all_to_all(codes, 'depth', 0, 0, tiled=True))  17.4 us
    all_to_all x2, waiting for transfers between devices, local(): sent.append(lax.all_to_all(codes, 'depth', 0, 0, tiled=True))  14.7 us
    pallas_call x2, Pallas kernels, merge(): pl.pallas_call(merge_kernel, grid=(1,), in_specs=specs, out_specs=here, o...  4.78 us
    ppermute x1, starting transfers between devices, local(): before = lax.ppermute(heat[-1], 'depth', on)  4.58 us
    ppermute x1, waiting for transfers between devices, local(): lower = lax.ppermute(heat[:, 0, :], 'cross', up)  2.06 us
  transfers between devices with their start and end apart: 6, of which 4 were waited for; matrix products, arithmetic and copies ran while one was open for 3% of the time, Pallas kernels for 25%

profile of v1, /device:TPU:0, one launch (start us, length us, event | category | flops | bytes accessed | tf_op | source)
XLA Modules:
  0.0 101.8 jit_solution(7864244735527217849)
XLA Ops:
  0.0 1.3 %slice_bitcast_fusion = (bf16[128,2048]{1,0:T(8,128)(2,1)S(1)}, bf16[128,2048]{1,0:T(8,128)(2,1)S(1)}) fusion(bf16[16,128,2048]{2,1,0:T(8,128)(2,1)} %below_ref.3), kind=kLoop, calls=%fused_computation | loop fusion | bytes 2097152 | tf_op jit(solution)/shard_map/squeeze | solution.py:233
  1.3 1.3 %collective-permute-start.1 = (bf16[128,2048]{1,0:T(8,128)(2,1)S(1)}, bf16[128,2048]{1,0:T(8,128)(2,1)S(1)}, u32[]{:S(2)}, u32[]{:S(2)}) collective-permute-start(bf16[128,2048]{1,0:T(8,128)(2,1)S(1)} %get-tuple-element.7), channel_id=1, source_target_pairs={{8,0},{16,8},{24,16},{32,24},{40,32},{48,40},{56,48},{64,56},{72,6... | collective-permute-start | bytes 1572872 | tf_op jit(solution)/shard_map/ppermute | solution.py:233
  2.6 4.6 %collective-permute-start = (bf16[128,2048]{1,0:T(8,128)(2,1)S(1)}, bf16[128,2048]{1,0:T(8,128)(2,1)S(1)}, u32[]{:S(2)}, u32[]{:S(2)}) collective-permute-start(bf16[128,2048]{1,0:T(8,128)(2,1)S(1)} %get-tuple-element.8), channel_id=1, source_target_pairs={{0,8},{8,16},{16,24},{24,32},{32,40},{40,48},{48,56},{56,64},{64,7... | collective-permute-start | bytes 1572872 | tf_op jit(solution)/shard_map/ppermute | solution.py:232
  7.2 1.4 %fusion = (bf16[16,1,2048]{2,1,0:T(2,128)(2,1)S(1)}, bf16[16,1,2048]{2,1,0:T(2,128)(2,1)S(1)}) fusion(bf16[16,128,2048]{2,1,0:T(8,128)(2,1)} %below_ref.3), kind=kLoop, calls=%fused_computation.5 | loop fusion | bytes 262144 | tf_op jit(solution)/shard_map/slice | solution.py:231
  8.6 1.3 %collective-permute-start.2 = (bf16[16,2048]{1,0:T(8,128)(2,1)S(1)}, bf16[16,2048]{1,0:T(8,128)(2,1)S(1)}, u32[]{:S(2)}, u32[]{:S(2)}) collective-permute-start(bf16[16,2048]{1,0:T(8,128)(2,1)S(1)} %bitcast.10), channel_id=1, source_target_pairs={{0,1},{1,2},{2,3},{3,4},{4,5},{5,6},{6,7},{8,9},{9,10},{10,11},{11... | collective-permute-start | bytes 196616 | tf_op jit(solution)/shard_map/ppermute | solution.py:230
  10.0 1.3 %collective-permute-start.3 = (bf16[16,2048]{1,0:T(8,128)(2,1)S(1)}, bf16[16,2048]{1,0:T(8,128)(2,1)S(1)}, u32[]{:S(2)}, u32[]{:S(2)}) collective-permute-start(bf16[16,2048]{1,0:T(8,128)(2,1)S(1)} %bitcast.11), channel_id=1, source_target_pairs={{1,0},{2,1},{3,2},{4,3},{5,4},{6,5},{7,6},{9,8},{10,9},{11,10},{12... | collective-permute-start | bytes 196616 | tf_op jit(solution)/shard_map/ppermute | solution.py:231
  11.3 0.7 slice.19
  12.0 0.7 slice.18
  12.7 0.6 pad.4.table_ref
  13.3 0.0 collective-permute-done.2.upper_ref
  13.3 2.1 %collective-permute-done.3.lower_ref = bf16[16,2048]{1,0:T(8,128)(2,1)S(1)} collective-permute-done((bf16[16,2048]{1,0:T(8,128)(2,1)S(1)}, bf16[16,2048]{1,0:T(8,128)(2,1)S(1)}, u32[]{:S(2)}, u32[]{:S(2)}) %collective-permute-start.3) | collective-permute-done | bytes 65568 | tf_op jit(solution)/shard_map/ppermute | solution.py:231
  15.4 1.3 %collective-permute-done.1.after_ref = bf16[128,2048]{1,0:T(8,128)(2,1)S(1)} collective-permute-done((bf16[128,2048]{1,0:T(8,128)(2,1)S(1)}, bf16[128,2048]{1,0:T(8,128)(2,1)S(1)}, u32[]{:S(2)}, u32[]{:S(2)}) %collective-permute-start.1) | collective-permute-done | bytes 524320 | tf_op jit(solution)/shard_map/ppermute | solution.py:233
  16.7 1.2 %collective-permute-done.before_ref = bf16[128,2048]{1,0:T(8,128)(2,1)S(1)} collective-permute-done((bf16[128,2048]{1,0:T(8,128)(2,1)S(1)}, bf16[128,2048]{1,0:T(8,128)(2,1)S(1)}, u32[]{:S(2)}, u32[]{:S(2)}) %collective-permute-start) | collective-permute-done | bytes 524320 | tf_op jit(solution)/shard_map/ppermute | solution.py:232
  17.9 0.0 copy-done.4
  17.9 0.8 copy-done.3
  18.7 22.6 %brick.3 = s16[16,4,64,128]{3,2,1,0:T(8,128)(2,1)} custom-call(s32[2,128]{1,0:T(2,128)} %pad.4.table_ref, bf16[512,256]{1,0:T(8,128)(2,1)} %constant.12.clone.diff_ref, bf16[16,128,2048]{2,1,0:T(8,128)(2,1)} %below_ref.3, bf16[16,128,2048]{2,1,0:T(8,128)(2,1)} %below_ref.3, bf16[16,128,2048]{2,1,0:T(8,128)(2,1)} %below_ref.3, ...), custom_call_target="tpu_custom_call" | custom-call | tf_op jit(solution)/shard_map/brick/pallas_call | solution.py:141
  41.3 10.1 %all-to-all-start.1 = ((s16[16,4,64,128]{3,2,1,0:T(8,128)(2,1)}), s16[16,4,64,128]{3,2,1,0:T(8,128)(2,1)S(1)}, u32[]{:S(2)}, u32[]{:S(2)}) async-start(s16[16,4,64,128]{3,2,1,0:T(8,128)(2,1)} %brick.3), calls=%async_computation.1 | async-start | bytes 2097152 | tf_op jit(solution)/shard_map/all_to_all | solution.py:239
  51.4 22.6 %brick.2 = s16[16,4,64,128]{3,2,1,0:T(8,128)(2,1)} custom-call(s32[2,128]{1,0:T(2,128)} %pad.4.table_ref, bf16[512,256]{1,0:T(8,128)(2,1)} %constant.12.clone.diff_ref, bf16[16,128,2048]{2,1,0:T(8,128)(2,1)} %below_ref.3, bf16[16,128,2048]{2,1,0:T(8,128)(2,1)} %below_ref.3, bf16[16,128,2048]{2,1,0:T(8,128)(2,1)} %below_ref.3, ...), custom_call_target="tpu_custom_call" | custom-call | tf_op jit(solution)/shard_map/brick/pallas_call | solution.py:141
  74.0 0.0 all-to-all-done.1.got_ref
  74.1 7.2 %all-to-all-start = ((s16[16,4,64,128]{3,2,1,0:T(8,128)(2,1)}), s16[16,4,64,128]{3,2,1,0:T(8,128)(2,1)S(1)}, u32[]{:S(2)}, u32[]{:S(2)}) async-start(s16[16,4,64,128]{3,2,1,0:T(8,128)(2,1)} %brick.2), calls=%async_computation | async-start | bytes 2097152 | tf_op jit(solution)/shard_map/all_to_all | solution.py:239
  81.3 2.4 %merge.2.rest_0_ = f32[4,128,128]{2,1,0:T(8,128)} custom-call(s16[16,4,64,128]{3,2,1,0:T(8,128)(2,1)} %copy-done), custom_call_target="tpu_custom_call" | custom-call | tf_op jit(solution)/shard_map/merge/pallas_call | solution.py:198
  83.7 14.7 %all-to-all-done.got_ref = s16[16,4,64,128]{3,2,1,0:T(8,128)(2,1)S(1)} async-done(((s16[16,4,64,128]{3,2,1,0:T(8,128)(2,1)}), s16[16,4,64,128]{3,2,1,0:T(8,128)(2,1)S(1)}, u32[]{:S(2)}, u32[]{:S(2)}) %all-to-all-start) | async-done | bytes 1048608 | tf_op jit(solution)/shard_map/all_to_all | solution.py:239
  98.4 1.0 copy-done.1
  99.4 2.4 %merge.3 = f32[4,128,128]{2,1,0:T(8,128)} custom-call(s16[16,4,64,128]{3,2,1,0:T(8,128)(2,1)} %copy-done.1, f32[4,128,128]{2,1,0:T(8,128)} %merge.2.rest_0_), custom_call_target="tpu_custom_call", output_to_operand_aliasing={{}: (1, {})} | custom-call | tf_op jit(solution)/shard_map/merge/pallas_call | solution.py:198
  (12 shorter events, 0.1 us)
Async XLA Ops:
  1.3 15.4 %collective-permute-start.1 = (bf16[128,2048]{1,0:T(8,128)(2,1)S(1)}, bf16[128,2048]{1,0:T(8,128)(2,1)S(1)}, u32[]{:S(2)}, u32[]{:S(2)}) collective-permute-start(bf16[128,2048]{1,0:T(8,128)(2,1)S(1)} %get-tuple-element.7), channel_id=1, source_target_pairs={{8,0},{16,8},{24,16},{32,24},{40,32},{48,40},{56,48},{64,56},{72,6... | collective-permute-start | bytes 1572872 | tf_op jit(solution)/shard_map/ppermute | solution.py:233
  2.6 15.3 %collective-permute-start = (bf16[128,2048]{1,0:T(8,128)(2,1)S(1)}, bf16[128,2048]{1,0:T(8,128)(2,1)S(1)}, u32[]{:S(2)}, u32[]{:S(2)}) collective-permute-start(bf16[128,2048]{1,0:T(8,128)(2,1)S(1)} %get-tuple-element.8), channel_id=1, source_target_pairs={{0,8},{8,16},{16,24},{24,32},{32,40},{40,48},{48,56},{56,64},{64,7... | collective-permute-start | bytes 1572872 | tf_op jit(solution)/shard_map/ppermute | solution.py:232
  8.6 4.7 %collective-permute-start.2 = (bf16[16,2048]{1,0:T(8,128)(2,1)S(1)}, bf16[16,2048]{1,0:T(8,128)(2,1)S(1)}, u32[]{:S(2)}, u32[]{:S(2)}) collective-permute-start(bf16[16,2048]{1,0:T(8,128)(2,1)S(1)} %bitcast.10), channel_id=1, source_target_pairs={{0,1},{1,2},{2,3},{3,4},{4,5},{5,6},{6,7},{8,9},{9,10},{10,11},{11... | collective-permute-start | bytes 196616 | tf_op jit(solution)/shard_map/ppermute | solution.py:230
  10.0 5.4 %collective-permute-start.3 = (bf16[16,2048]{1,0:T(8,128)(2,1)S(1)}, bf16[16,2048]{1,0:T(8,128)(2,1)S(1)}, u32[]{:S(2)}, u32[]{:S(2)}) collective-permute-start(bf16[16,2048]{1,0:T(8,128)(2,1)S(1)} %bitcast.11), channel_id=1, source_target_pairs={{1,0},{2,1},{3,2},{4,3},{5,4},{6,5},{7,6},{9,8},{10,9},{11,10},{12... | collective-permute-start | bytes 196616 | tf_op jit(solution)/shard_map/ppermute | solution.py:231
  13.3 4.6 %copy-start.4 = (bf16[16,2048]{1,0:T(8,128)(2,1)}, bf16[16,2048]{1,0:T(8,128)(2,1)S(1)}, u32[]{:S(2)}) copy-start(bf16[16,2048]{1,0:T(8,128)(2,1)S(1)} %collective-permute-done.2.upper_ref) | copy-start | bytes 196612
  15.4 2.5 %copy-start.5 = (bf16[16,2048]{1,0:T(8,128)(2,1)}, bf16[16,2048]{1,0:T(8,128)(2,1)S(1)}, u32[]{:S(2)}) copy-start(bf16[16,2048]{1,0:T(8,128)(2,1)S(1)} %collective-permute-done.3.lower_ref) | copy-start | bytes 196612
  16.7 1.2 %copy-start.2 = (bf16[128,2048]{1,0:T(8,128)(2,1)}, bf16[128,2048]{1,0:T(8,128)(2,1)S(1)}, u32[]{:S(2)}) copy-start(bf16[128,2048]{1,0:T(8,128)(2,1)S(1)} %collective-permute-done.1.after_ref) | copy-start | bytes 1572868
  17.9 0.8 copy-start.3
  41.3 32.8 %all-to-all-start.1 = ((s16[16,4,64,128]{3,2,1,0:T(8,128)(2,1)}), s16[16,4,64,128]{3,2,1,0:T(8,128)(2,1)S(1)}, u32[]{:S(2)}, u32[]{:S(2)}) async-start(s16[16,4,64,128]{3,2,1,0:T(8,128)(2,1)} %brick.3), calls=%async_computation.1 | async-start | bytes 2097152 | tf_op jit(solution)/shard_map/all_to_all | solution.py:239
  74.1 7.2 %copy-start = (s16[16,4,64,128]{3,2,1,0:T(8,128)(2,1)}, s16[16,4,64,128]{3,2,1,0:T(8,128)(2,1)S(1)}, u32[]{:S(2)}) copy-start(s16[16,4,64,128]{3,2,1,0:T(8,128)(2,1)S(1)} %all-to-all-done.1.got_ref) | copy-start | bytes 3145732
  74.1 24.3 %all-to-all-start = ((s16[16,4,64,128]{3,2,1,0:T(8,128)(2,1)}), s16[16,4,64,128]{3,2,1,0:T(8,128)(2,1)S(1)}, u32[]{:S(2)}, u32[]{:S(2)}) async-start(s16[16,4,64,128]{3,2,1,0:T(8,128)(2,1)} %brick.2), calls=%async_computation | async-start | bytes 2097152 | tf_op jit(solution)/shard_map/all_to_all | solution.py:239
  98.4 1.0 copy-start.1

commit v2 on v0

v2 whole, which is shorter than its diff:
```python
import jax
import jax.numpy as jnp
import numpy as np
from jax import lax
from jax.experimental import pallas as pl
from jax.experimental.pallas import tpu as pltpu
from jax.sharding import PartitionSpec as P

LANES = 128
SUBLANES = 8
PIECE = 256
f32 = jnp.float32
LANE_LOOKUP = lax.GatherDimensionNumbers(
    offset_dims=(),
    collapsed_slice_dims=(1,),
    start_index_map=(1,),
    operand_batching_dims=(0,),
    start_indices_batching_dims=(0,),
)
KAPPA = -2.0 / float(np.log(2.0))
HIGH_STEPS = 32766.0
LOW_STEPS = 65535.0
CENTRE = 16.0
STEPS = 2340.0
LEAST = 2.0**-29.9


def strip_pipeline(table_ref, rims_ref, before_ref, after_ref, heat_hbm, entry_hbm, state_ref, out_ref, diff, heat, entry,
                   rim_rows, ta, da, tb, db, heat_sem, entry_sem, *, segments, mode, sight):
    all_rows, columns = heat_hbm.shape[1:]
    layers = heat_hbm.shape[0]
    height = segments[0][1]
    count = columns // PIECE
    strips = PIECE // LANES
    if mode == "all":
        centres, shift, extras = list(range(1, layers + 1)), 1, {0: "before", layers + 1: "after"}
    elif mode == "mid":
        centres, shift, extras = list(range(1, layers - 1)), 0, {0: 0, layers - 1: layers - 1}
    else:
        centres, shift, extras = [1, 4], 1, {0: "before", 2: 1, 3: 2, 5: "after"}
    stride = centres[1] - centres[0]
    parts = strips if height > 16 else 1
    share = len(centres) // parts
    batch = min(share, 128 // height)
    while share % batch:
        batch -= 1
    units_at_once = 4 if height % 32 == 0 else 2

    def heat_copies(p):
        cols = pl.ds(pl.multiple_of(p * PIECE, PIECE), PIECE)
        into = pl.ds(pl.multiple_of(2 * LANES + p * PIECE, LANES), PIECE)
        found = []
        for k, (row, _) in enumerate(segments):
            low, high = max(row - 16, 0), min(row + height + 16, all_rows)
            target = pl.ds(16 - (row - low), high - low)
            if mode == "ends":
                pairs = [(0, 0, 2), (layers - 2, 2, 2)]
            else:
                pairs = [(0, 0, layers)]
            for n, (source, first, size) in enumerate(pairs):
                found.append(
                    pltpu.make_async_copy(
                        heat_hbm.at[pl.ds(source, size), pl.ds(low, high - low), cols],
                        heat.at[k, pl.ds(first, size), target, into],
                        heat_sem.at[2 * k + n, p],
                    )
                )
        return found

    def entry_copies(p):
        cols = pl.ds(pl.multiple_of(p * PIECE, PIECE), PIECE)
        found = []
        for k, (row, _) in enumerate(segments):
            if mode == "ends":
                pairs = [(0, 0, 1), (layers - 1, 1, 1)]
            else:
                pairs = [(1 if mode == "mid" else 0, 0, len(centres))]
            for n, (source, first, size) in enumerate(pairs):
                found.append(
                    pltpu.make_async_copy(
                        entry_hbm.at[pl.ds(source, size), pl.ds(row, height), cols],
                        entry.at[pl.ds(first, size), pl.ds(k * height, height), cols],
                        entry_sem.at[2 * k + n, p],
                    )
                )
        return found

    def start(copies):
        for copy in copies:
            copy.start()

    def wait(copies):
        for copy in copies:
            copy.wait()

    start(heat_copies(0))
    start(heat_copies(1))
    for p in range(count):
        start(entry_copies(p))
        if p + 2 < count:
            start(heat_copies(p + 2))

    heat[:, :, :, 0 : 2 * LANES] = jnp.zeros(heat.shape[:3] + (2 * LANES,), jnp.bfloat16)
    heat[:, :, :, 2 * LANES + columns :] = jnp.zeros(heat.shape[:3] + (LANES,), jnp.bfloat16)
    k = lax.broadcasted_iota(jnp.int32, diff.shape, 0) - lax.broadcasted_iota(jnp.int32, diff.shape, 1)
    diff[...] = jnp.where(k == LANES + 1, 1.0, jnp.where(k == LANES - 1, -1.0, 0.0)).astype(jnp.bfloat16)
    if rims_ref is not None:
        rim_rows[...] = rims_ref[...].astype(f32)

    def prepare(p, seg, t, dv, n, qs):
        row = segments[seg][0]
        own = pl.ds(pl.multiple_of(p * PIECE, PIECE), PIECE)
        cols = pl.ds(pl.multiple_of(2 * LANES + p * PIECE, LANES), PIECE)
        wide = pl.ds(pl.multiple_of(LANES + p * PIECE, LANES), PIECE + 2 * LANES)
        mid = slice(16, 16 + height)

        def put(slot, first, value):
            for q in range(strips):
                t[q, slot, first : first + value.shape[0], :] = value[:, q * LANES : (q + 1) * LANES]

        for q in qs:
            for slot, source in extras.items():
                here = pl.multiple_of(p * PIECE + q * LANES, LANES)
                if source == "before":
                    value = before_ref[row : row + height, pl.ds(here, LANES)]
                elif source == "after":
                    value = after_ref[row : row + height, pl.ds(here, LANES)]
                else:
                    value = heat[seg, source, mid, pl.ds(2 * LANES + here, LANES)]
                t[q, slot, 8 : 8 + height, :] = value.astype(f32)
        for first in range(0, share, batch):
            at = n * share + first
            slot0 = centres[0] + stride * at
            if stride == 1:
                window = heat[seg, pl.ds(slot0 - shift, batch), mid, wide].reshape(batch * height, PIECE + 2 * LANES)
            else:
                window = jnp.concatenate([heat[seg, centres[0] - shift + stride * (at + m), mid, wide] for m in range(batch)], axis=0)
            moved = jnp.dot(window, diff[...], preferred_element_type=f32).reshape(batch, height, PIECE)
            for q in range(strips):
                dv[q, pl.ds(at, batch)] = moved[:, :, q * LANES : (q + 1) * LANES]
            for m in range(batch):
                slot = slot0 + stride * m
                z = slot - shift
                layer = z if mode != "ends" else jnp.where(at + m == 0, 0, layers - 1)
                put(slot, 8, heat[seg, z, mid, cols].astype(f32))
                if row == 0:
                    put(slot, 7, rim_rows[0, pl.ds(layer, 1), own])
                else:
                    put(slot, 0, heat[seg, z, 0:16, cols].astype(f32)[8:16])
                if row + height == all_rows:
                    put(slot, 8 + height, rim_rows[1, pl.ds(layer, 1), own])
                else:
                    put(slot, 8 + height, heat[seg, z, 16 + height : 32 + height, cols].astype(f32)[0:8])
                yield

    tables = []
    for pair in range(2):
        low_half = jnp.round(table_ref[2 * pair + 1 : 2 * pair + 2, :] * LOW_STEPS)
        high_half = jnp.round(table_ref[2 * pair : 2 * pair + 1, :] * HIGH_STEPS - low_half * (1.0 / 65536.0))
        words = high_half.astype(jnp.int32) * 65536 + low_half.astype(jnp.int32)
        tables.append(jnp.broadcast_to(words, (SUBLANES, LANES)))

    def looked(index):
        rg, ba = [
            lax.gather(table, index[:, :, None], LANE_LOOKUP, (1, 1), mode=lax.GatherScatterMode.PROMISE_IN_BOUNDS)
            for table in tables
        ]
        return rg.astype(f32), (rg & 0xFFFF).astype(f32), ba.astype(f32), (ba & 0xFFFF).astype(f32) * (4.0 / (sight * LOW_STEPS))

    scale = 0.7 / 9.0
    scales = [scale / (HIGH_STEPS * 65536.0), scale / LOW_STEPS, scale / (HIGH_STEPS * 65536.0)]

    def composite(p, seg, t, dv, qs):
        jobs = [(q, r0) for q in qs for r0 in range(0, height, SUBLANES)]
        size = units_at_once if parts > 1 else len(jobs)
        for group in range(0, len(jobs), size):
            units = []
            for q, r0 in jobs[group : group + size]:
                s = strips * p + q
                units.append(
                    dict(
                        q=q,
                        s=s,
                        r0=r0,
                        cols=pl.ds(pl.multiple_of(s * LANES, LANES), LANES),
                        trans=jnp.ones((SUBLANES, LANES), f32),
                        colors=[jnp.zeros((SUBLANES, LANES), f32) for channel in range(3)],
                        prev=t[q, centres[0] - 1, 8 + r0 : 16 + r0, :],
                        cur=t[q, centres[0], 8 + r0 : 16 + r0, :],
                    )
                )
            for at, slot in enumerate(centres):
                for unit in units:
                    q, r0 = unit["q"], unit["r0"]
                    if mode == "ends" and at == 1:
                        kept = [state_ref[unit["s"], channel, seg * height + r0 : seg * height + r0 + 8, :] for channel in range(4)]
                        unit["colors"] = [old + unit["trans"] * new for old, new in zip(unit["colors"], kept)]
                        unit["trans"] = unit["trans"] * kept[3]
                        unit["prev"], unit["cur"] = t[q, slot - 1, 8 + r0 : 16 + r0, :], t[q, slot, 8 + r0 : 16 + r0, :]
                    nxt = t[q, slot + 1, 8 + r0 : 16 + r0, :]
                    a = nxt - unit["prev"]
                    b = t[q, slot, 9 + r0 : 17 + r0, :] - t[q, slot, 7 + r0 : 15 + r0, :]
                    c = dv[q, at, r0 : r0 + 8, :]
                    m = b + c
                    lit = a + m + m
                    square = (a * a + b * b) + (c * c + 4.0)
                    shade = lit * lit * pl.reciprocal(square, approx=True) + 0.3 / scale
                    red, green, blue, weight = looked(entry[at, seg * height + r0 : seg * height + r0 + 8, unit["cols"]])
                    alpha = weight * pl.reciprocal(jnp.exp2(unit["cur"] * KAPPA) + 1.0, approx=True)
                    part = alpha * unit["trans"]
                    unit["trans"] = unit["trans"] - part
                    shown = shade * part
                    unit["colors"] = [old + new * shown for old, new in zip(unit["colors"], (red, green, blue))]
                    unit["prev"], unit["cur"] = unit["cur"], nxt
                yield
            for pair in range(0, len(units), 2):
                twin = units[pair : pair + 2]
                r0 = seg * height + twin[0]["r0"]
                for channel in range(4):
                    if mode == "mid":
                        values = [unit["colors"][channel] if channel < 3 else unit["trans"] for unit in twin]
                        out_ref[twin[0]["s"], channel, r0 : r0 + 16, :] = jnp.concatenate(values, axis=0)
                        continue
                    values = [unit["colors"][channel] * scales[channel] if channel < 3 else 1.0 - unit["trans"] for unit in twin]
                    code = jnp.round((jnp.log2(jnp.maximum(jnp.concatenate(values, axis=0), LEAST)) + CENTRE) * STEPS)
                    out_ref[twin[0]["s"], channel, r0 : r0 + 16, :] = code.astype(jnp.int32).astype(jnp.int16)

    def both(first, second):
        def part(n, carry):
            qs = [n] if parts > 1 else list(range(strips))
            following = prepare(*second, n, qs)
            groups = max(height // (SUBLANES * units_at_once), 1) if parts > 1 else 1
            steps = max(groups * len(centres) // share, 1)
            for at, step in enumerate(composite(*first, qs)):
                if at % steps == 0:
                    next(following, None)
            for step in following:
                pass
            return carry

        if parts > 1:
            lax.fori_loop(0, parts, part, 0)
        else:
            part(0, 0)

    wait(heat_copies(0))
    wait(heat_copies(1))
    for n in range(parts):
        for step in prepare(0, 0, ta, da, n, [n] if parts > 1 else list(range(strips))):
            pass

    def body(i, carry):
        @pl.when(i + 2 < count)
        def _():
            wait(heat_copies(i + 2))

        wait(entry_copies(i))
        both((i, 0, ta, da), (i, 1, tb, db))
        both((i, 1, tb, db), (jnp.minimum(i + 1, count - 1), 0, ta, da))
        return carry

    lax.fori_loop(0, count, body, 0)


def brick(table, heat, entry, segments, mode, sight, before=None, after=None, rims=None, state=None, codes=None, out_rows=None):
    layers, all_rows, columns = heat.shape
    height = segments[0][1]
    own_rows = 2 * height
    out_rows = out_rows or own_rows
    blocks = columns // LANES
    whole = pl.BlockSpec(memory_space=pl.ANY)
    given = {"table": (table, pl.BlockSpec((4, LANES), lambda i: (0, 0))), "heat": (heat, whole), "entry": (entry, whole)}
    if rims is not None:
        given["rims"] = (rims, pl.BlockSpec(rims.shape, lambda i: (0, 0, 0)))
    if before is not None:
        given["before"] = (before, pl.BlockSpec(before.shape, lambda i: (0, 0)))
        given["after"] = (after, pl.BlockSpec(after.shape, lambda i: (0, 0)))
    if state is not None:
        given["state"] = (state, pl.BlockSpec(state.shape, lambda i: (0, 0, 0, 0)))
    if codes is not None:
        given["codes"] = (codes, whole)
    names = list(given)
    held, centres = {"all": (layers, layers), "mid": (layers, layers - 2), "ends": (4, 2)}[mode]
    slots = {"all": layers + 2, "mid": layers, "ends": 6}[mode]
    t = pltpu.VMEM((PIECE // LANES, slots, height + 16, LANES), f32)
    dv = pltpu.VMEM((PIECE // LANES, centres, height, LANES), f32)

    def kernel(*refs):
        ref = dict(zip(names, refs))
        rest = refs[len(names) :]
        strip_pipeline(ref["table"], ref.get("rims"), ref.get("before"), ref.get("after"), ref["heat"], ref["entry"],
                       ref.get("state"), *rest, segments=segments, mode=mode, sight=sight)

    return pl.pallas_call(
        kernel,
        grid=(1,),
        in_specs=[given[name][1] for name in names],
        out_specs=pl.BlockSpec((blocks, 4, own_rows, LANES), lambda i: (0, 0, 0 if codes is None else 1, 0)),
        out_shape=jax.ShapeDtypeStruct((blocks, 4, out_rows, LANES), f32 if mode == "mid" else jnp.int16),
        scratch_shapes=[
            pltpu.VMEM((PIECE + 2 * LANES, PIECE), jnp.bfloat16),
            pltpu.VMEM((2, held, height + 32, columns + 3 * LANES), jnp.bfloat16),
            pltpu.VMEM((centres, own_rows, columns), jnp.int32),
            pltpu.VMEM((2, layers, columns), f32),
            t,
            dv,
            t,
            dv,
            pltpu.SemaphoreType.DMA((4, columns // PIECE)),
            pltpu.SemaphoreType.DMA((4, columns // PIECE)),
        ],
        input_output_aliases={} if codes is None else {names.index("codes"): 0},
        compiler_params=pltpu.CompilerParams(vmem_limit_bytes=44 * 1024 * 1024),
        name=mode + "_layers",
    )(*[given[name][0] for name in names])


def merge_kernel(got_ref, *rest):
    out_ref = rest[-1]
    count, channels, rows, lanes = got_ref.shape
    colors = [jnp.zeros((rows, lanes), f32) for channel in range(3)]
    trans = jnp.ones((rows, lanes), f32)
    for source in range(count):
        value = [jnp.exp2(got_ref[source, channel].astype(f32) * (1.0 / STEPS) - CENTRE) for channel in range(4)]
        colors = [old + trans * new for old, new in zip(colors, value)]
        trans = trans - trans * value[3]
    for channel in range(4):
        out_ref[channel] = colors[channel] if channel < 3 else 1.0 - trans


def merge(got, image, all_rows, place):
    count, channels, rows, lanes = got.shape
    operands, specs, aliases = [got], [pl.BlockSpec((count, channels, 16, lanes), lambda i: (0, 0, i, 0))], {}
    if image is not None:
        operands.append(image)
        specs.append(pl.BlockSpec(memory_space=pl.ANY))
        aliases = {1: 0}
    return pl.pallas_call(
        merge_kernel,
        grid=(rows // 16,),
        in_specs=specs,
        out_specs=pl.BlockSpec((channels, 16, lanes), lambda i: (0, place(i), 0)),
        out_shape=jax.ShapeDtypeStruct((channels, all_rows, lanes), f32),
        input_output_aliases=aliases,
        name="merge",
    )(*operands)


def local(heat, entry, table):
    count = lax.axis_size("depth")
    sides = lax.axis_size("cross")
    layers, rows, columns = heat.shape
    sight = layers * count
    on, back = [(i, i + 1) for i in range(count - 1)], [(i + 1, i) for i in range(count - 1)]
    before = lax.ppermute(heat[-1], "depth", on)
    after = lax.ppermute(heat[0], "depth", back)
    mine = jnp.stack([heat[:, -1, :], heat[:, 0, :]])
    every = lax.all_gather(mine, "cross", axis=0)
    me = lax.axis_index("cross")
    upper = lax.dynamic_index_in_dim(every, jnp.maximum(me - 1, 0), 0, keepdims=False)[0]
    lower = lax.dynamic_index_in_dim(every, jnp.minimum(me + 1, sides - 1), 0, keepdims=False)[1]
    nothing = jnp.zeros((), heat.dtype)
    rims = jnp.stack([jnp.where(me > 0, upper, nothing), jnp.where(me < sides - 1, lower, nothing)])
    table = jnp.pad(table, ((0, 0), (0, LANES - table.shape[1])))

    centre, inner, outer = ((48, 16), (64, 16)), ((16, 32), (80, 32)), ((0, 16), (112, 16))
    state = brick(table, heat, entry, centre, "mid", sight)
    codes = brick(table, heat, entry, inner, "all", sight, before=before, after=after)
    first = lax.all_to_all(codes, "depth", 0, 0, tiled=True)
    codes = brick(table, heat, entry, outer, "all", sight, before=before, after=after, rims=rims, out_rows=64)
    codes = brick(table, heat, entry, centre, "ends", sight, before=before, after=after, state=state, codes=codes, out_rows=64)
    second = lax.all_to_all(codes, "depth", 0, 0, tiled=True)
    image = merge(first, None, rows, lambda i: i + 1 + 2 * (i // 2))
    return merge(second, image, rows, lambda i: jnp.where(i == 0, 0, jnp.where(i == 1, 7, i + 1)))


def solution(mesh):
    in_specs = (P("depth", "cross", None), P("depth", "cross", None), P())
    out_specs = P(None, "cross", "depth")
    return jax.shard_map(local, mesh=mesh, in_specs=in_specs, out_specs=out_specs, check_vma=False)
```

time: 439 us -> 117 us (0.27)
  other arithmetic: 273 us -> 1.58 us
  waiting for transfers between devices: 90.3 us -> 22.4 us
  Pallas kernels: 0 us -> 47.5 us
  local copies, waits for them, and re-layouts: 49.8 us -> 7.81 us
  between operations: 0.22 us -> 13.5 us
    reduce_sum x3 -> x0, other arithmetic: 161 us -> none  [local(): jnp.sum(looked[channel] * weight, axis=0)]
    ppermute x8 -> x2, waiting for transfers between devices: 90.3 us -> 10 us  [the longest x1 8.82 us: local(): after = lax.ppermute(heat[0], 'depth', back)]
    mul x5 -> x0, other arithmetic: 72.8 us -> none  [the longest x1 72.7 us: local(): alpha = scale_alpha * looked[3] * jax.nn.sigmoid(2.0 * centre)]
    pallas_call x0 -> x6, Pallas kernels: none -> 47.5 us  [the longest x4 40.6 us: brick(): pl.pallas_call(kernel, grid=(1,), in_specs=[given[name][1] for name in na...]
    slice x9 -> x1, local copies, waits for them, and re-layouts: 23.7 us -> 1.41 us  [local(): mine = jnp.stack([heat[:, -1, :], heat[:, 0, :]])]
    ppermute x8 -> x2, starting transfers between devices: 23.6 us -> 5.87 us  [the longest x1 4.58 us: local(): before = lax.ppermute(heat[-1], 'depth', on)]
    all_to_all x0 -> x2, starting transfers between devices: none -> 17.4 us  [the longest x1 10.1 us: local(): first = lax.all_to_all(codes, 'depth', 0, 0, tiled=True)]
    convert_element_type x1 -> x0, other arithmetic: 13.7 us -> none  [local(): haloed_heat_mesh.astype(jnp.float32)]
  transfers between devices with their start and end apart: 8 -> 5, of which waited for: 6 -> 3; matrix products, arithmetic and copies ran while one was open for 4% -> 2% of each run, Pallas kernels for 0% -> 38%
where the time goes in v2:
time: 117 us; the launch traced here: 116 us
  Pallas kernels  47.5 us (41%)
  starting transfers between devices  23.2 us (20%)
  waiting for transfers between devices  22.4 us (19%)
  between operations  13.5 us (12%)
  local copies, waits for them, and re-layouts  7.81 us (7%)
  other arithmetic  1.58 us (1%)
    pallas_call x4, Pallas kernels, brick(): pl.pallas_call(kernel, grid=(1,), in_specs=[given[name][1] for name in na...  40.6 us
    all_to_all x1, waiting for transfers between devices, local(): second = lax.all_to_all(codes, 'depth', 0, 0, tiled=True)  12.4 us
    all_to_all x1, starting transfers between devices, local(): first = lax.all_to_all(codes, 'depth', 0, 0, tiled=True)  10.1 us
    ppermute x1, waiting for transfers between devices, local(): after = lax.ppermute(heat[0], 'depth', back)  8.82 us
    all_to_all x1, starting transfers between devices, local(): second = lax.all_to_all(codes, 'depth', 0, 0, tiled=True)  7.22 us
    pallas_call x2, Pallas kernels, merge(): pl.pallas_call(merge_kernel, grid=(rows // 16,), in_specs=specs, out_spec...  6.86 us
    ppermute x1, starting transfers between devices, local(): before = lax.ppermute(heat[-1], 'depth', on)  4.58 us
    unnamed x6, local copies, waits for them, and re-layouts  4.36 us
  transfers between devices with their start and end apart: 5, of which 3 were waited for; matrix products, arithmetic and copies ran while one was open for 2% of the time, Pallas kernels for 38%

profile of v2, /device:TPU:0, one launch (start us, length us, event | category | flops | bytes accessed | tf_op | source)
XLA Modules:
  0.0 116.0 jit_solution(12528653259972848073)
XLA Ops:
  6.5 1.4 %fusion.2 = (bf16[16,1,2048]{2,1,0:T(2,128)(2,1)S(1)}, bf16[16,1,2048]{2,1,0:T(2,128)(2,1)S(1)}) fusion(bf16[16,128,2048]{2,1,0:T(8,128)(2,1)} %refs_1_.7), kind=kLoop, calls=%fused_computation.10 | loop fusion | bytes 262144 | tf_op jit(solution)/shard_map/slice | solution.py:357
  8.0 0.1 copy_bitcast_fusion
  8.0 0.7 pad_maximum_fusion
  8.7 0.0 all-gather.3.cloned.1.call-update
  8.7 1.3 %slice_bitcast_fusion = (bf16[128,2048]{1,0:T(8,128)(2,1)S(1)}, bf16[128,2048]{1,0:T(8,128)(2,1)S(1)}) fusion(bf16[16,128,2048]{2,1,0:T(8,128)(2,1)} %refs_1_.7), kind=kLoop, calls=%fused_computation | loop fusion | bytes 2097152 | tf_op jit(solution)/shard_map/squeeze | solution.py:356
  10.0 1.3 %collective-permute-start.1 = (bf16[128,2048]{1,0:T(8,128)(2,1)S(1)}, bf16[128,2048]{1,0:T(8,128)(2,1)S(1)}, u32[]{:S(2)}, u32[]{:S(2)}) collective-permute-start(bf16[128,2048]{1,0:T(8,128)(2,1)S(1)} %get-tuple-element.7), channel_id=1, source_target_pairs={{8,0},{16,8},{24,16},{32,24},{40,32},{48,40},{56,48},{64,56},{72,6... | collective-permute-start | bytes 1572872 | tf_op jit(solution)/shard_map/ppermute | solution.py:356
  11.3 4.6 %collective-permute-start = (bf16[128,2048]{1,0:T(8,128)(2,1)S(1)}, bf16[128,2048]{1,0:T(8,128)(2,1)S(1)}, u32[]{:S(2)}, u32[]{:S(2)}) collective-permute-start(bf16[128,2048]{1,0:T(8,128)(2,1)S(1)} %get-tuple-element.8), channel_id=1, source_target_pairs={{0,8},{8,16},{16,24},{24,32},{32,40},{40,48},{48,56},{56,64},{64,7... | collective-permute-start | bytes 1572872 | tf_op jit(solution)/shard_map/ppermute | solution.py:355
  15.9 0.7 pad.4.refs_0_
  16.6 8.8 %collective-permute-done.1.refs_5_.refs_4_ = bf16[128,2048]{1,0:T(8,128)(2,1)S(1)} collective-permute-done((bf16[128,2048]{1,0:T(8,128)(2,1)S(1)}, bf16[128,2048]{1,0:T(8,128)(2,1)S(1)}, u32[]{:S(2)}, u32[]{:S(2)}) %collective-permute-start.1) | collective-permute-done | bytes 524320 | tf_op jit(solution)/shard_map/ppermute | solution.py:356
  25.4 1.2 %collective-permute-done.refs_4_.refs_3_ = bf16[128,2048]{1,0:T(8,128)(2,1)S(1)} collective-permute-done((bf16[128,2048]{1,0:T(8,128)(2,1)S(1)}, bf16[128,2048]{1,0:T(8,128)(2,1)S(1)}, u32[]{:S(2)}, u32[]{:S(2)}) %collective-permute-start) | collective-permute-done | bytes 524320 | tf_op jit(solution)/shard_map/ppermute | solution.py:355
  26.6 18.0 %all_layers.3 = s16[16,4,64,128]{3,2,1,0:T(8,128)(2,1)} custom-call(f32[4,128]{1,0:T(4,128)S(1)} %pad.4.refs_0_, bf16[16,128,2048]{2,1,0:T(8,128)(2,1)} %refs_1_.7, s32[16,128,2048]{2,1,0:T(8,128)} %refs_2_.7, bf16[128,2048]{1,0:T(8,128)(2,1)S(1)} %collective-permute-done.refs_4_.refs_3_, bf16[128,2048]{1,0:T(8,128)(2,1)S(1)} %collective-permute-done.1.refs_5_.refs_4_), custom_call_target="tpu_custom_call" | custom-call | tf_op jit(solution)/shard_map/all_layers/pallas_call | solution.py:294
  44.6 10.1 %all-to-all-start.1 = ((s16[16,4,64,128]{3,2,1,0:T(8,128)(2,1)}), s16[16,4,64,128]{3,2,1,0:T(8,128)(2,1)S(1)}, u32[]{:S(2)}, u32[]{:S(2)}) async-start(s16[16,4,64,128]{3,2,1,0:T(8,128)(2,1)} %all_layers.3), calls=%async_computation.1 | async-start | bytes 2097152 | tf_op jit(solution)/shard_map/all_to_all | solution.py:369
  54.8 0.0 copy-start
  54.8 3.4 %copy-done = bf16[16,128,2048]{2,1,0:T(8,128)(2,1)S(1)} copy-done((bf16[16,128,2048]{2,1,0:T(8,128)(2,1)S(1)}, bf16[16,128,2048]{2,1,0:T(8,128)(2,1)}, u32[]{:S(2)}) %copy-start) | copy-done | bytes 8388632
  58.2 7.8 %mid_layers.1.refs_5_ = f32[16,4,32,128]{3,2,1,0:T(8,128)S(1)} custom-call(f32[4,128]{1,0:T(4,128)S(1)} %pad.4.refs_0_, bf16[16,128,2048]{2,1,0:T(8,128)(2,1)S(1)} %copy-done, s32[16,128,2048]{2,1,0:T(8,128)} %refs_2_.7), custom_call_target="tpu_custom_call" | custom-call | tf_op jit(solution)/shard_map/mid_layers/pallas_call | solution.py:294
  66.0 0.0 all-gather.3.cloned.1.call-done
  66.0 0.9 fusion.1
  67.0 10.2 %all_layers.2.refs_6_ = s16[16,4,64,128]{3,2,1,0:T(8,128)(2,1)} custom-call(f32[4,128]{1,0:T(4,128)S(1)} %pad.4.refs_0_, bf16[16,128,2048]{2,1,0:T(8,128)(2,1)} %refs_1_.7, s32[16,128,2048]{2,1,0:T(8,128)} %refs_2_.7, bf16[2,16,2048]{2,1,0:T(8,128)(2,1)S(1)} %pad_maximum_fusion.1.refs_3_, bf16[128,2048]{1,0:T(8,128)(2,1)S(1)} %collective-permute-done.refs_4_.refs_3_, ...), custom_call_target="tpu_custom_call" | custom-call | tf_op jit(solution)/shard_map/all_layers/pallas_call | solution.py:294
  77.1 4.6 %ends_layers.1 = s16[16,4,64,128]{3,2,1,0:T(8,128)(2,1)} custom-call(f32[4,128]{1,0:T(4,128)S(1)} %pad.4.refs_0_, bf16[16,128,2048]{2,1,0:T(8,128)(2,1)} %refs_1_.7, s32[16,128,2048]{2,1,0:T(8,128)} %refs_2_.7, bf16[128,2048]{1,0:T(8,128)(2,1)S(1)} %collective-permute-done.refs_4_.refs_3_, ...), custom_call_target="tpu_custom_call", output_to_operand_aliasing={{}: (6, {})} | custom-call | tf_op jit(solution)/shard_map/ends_layers/pallas_call | solution.py:294
  81.8 7.2 %all-to-all-start = ((s16[16,4,64,128]{3,2,1,0:T(8,128)(2,1)}), s16[16,4,64,128]{3,2,1,0:T(8,128)(2,1)S(1)}, u32[]{:S(2)}, u32[]{:S(2)}) async-start(s16[16,4,64,128]{3,2,1,0:T(8,128)(2,1)} %ends_layers.1), calls=%async_computation | async-start | bytes 2097152 | tf_op jit(solution)/shard_map/all_to_all | solution.py:372
  89.0 3.4 %merge.2.rest_0_ = f32[4,128,128]{2,1,0:T(8,128)} custom-call(s16[16,4,64,128]{3,2,1,0:T(8,128)(2,1)} %copy-done.1), custom_call_target="tpu_custom_call" | custom-call | tf_op jit(solution)/shard_map/merge/pallas_call | solution.py:338
  92.4 12.4 %all-to-all-done.got_ref = s16[16,4,64,128]{3,2,1,0:T(8,128)(2,1)S(1)} async-done(((s16[16,4,64,128]{3,2,1,0:T(8,128)(2,1)}), s16[16,4,64,128]{3,2,1,0:T(8,128)(2,1)S(1)}, u32[]{:S(2)}, u32[]{:S(2)}) %all-to-all-start) | async-done | bytes 1048608 | tf_op jit(solution)/shard_map/all_to_all | solution.py:372
  104.8 1.0 copy-done.2
  105.8 3.4 %merge.3 = f32[4,128,128]{2,1,0:T(8,128)} custom-call(s16[16,4,64,128]{3,2,1,0:T(8,128)(2,1)} %copy-done.2, f32[4,128,128]{2,1,0:T(8,128)} %merge.2.rest_0_), custom_call_target="tpu_custom_call", output_to_operand_aliasing={{}: (1, {})} | custom-call | tf_op jit(solution)/shard_map/merge/pallas_call | solution.py:338
  (6 shorter events, 0.0 us)
Async XLA Ops:
  6.5 59.5 %all-gather.3.cloned.1.call-start = ((), (), s32[]{:S(2)}) async-start(), calls=%async_computation.2 | async-start | bytes 1179648 | tf_op jit(solution)/shard_map/all_gather | solution.py:358
  10.0 15.4 %collective-permute-start.1 = (bf16[128,2048]{1,0:T(8,128)(2,1)S(1)}, bf16[128,2048]{1,0:T(8,128)(2,1)S(1)}, u32[]{:S(2)}, u32[]{:S(2)}) collective-permute-start(bf16[128,2048]{1,0:T(8,128)(2,1)S(1)} %get-tuple-element.7), channel_id=1, source_target_pairs={{8,0},{16,8},{24,16},{32,24},{40,32},{48,40},{56,48},{64,56},{72,6... | collective-permute-start | bytes 1572872 | tf_op jit(solution)/shard_map/ppermute | solution.py:356
  11.3 15.3 %collective-permute-start = (bf16[128,2048]{1,0:T(8,128)(2,1)S(1)}, bf16[128,2048]{1,0:T(8,128)(2,1)S(1)}, u32[]{:S(2)}, u32[]{:S(2)}) collective-permute-start(bf16[128,2048]{1,0:T(8,128)(2,1)S(1)} %get-tuple-element.8), channel_id=1, source_target_pairs={{0,8},{8,16},{16,24},{24,32},{32,40},{40,48},{48,56},{56,64},{64,7... | collective-permute-start | bytes 1572872 | tf_op jit(solution)/shard_map/ppermute | solution.py:355
  44.6 37.1 %all-to-all-start.1 = ((s16[16,4,64,128]{3,2,1,0:T(8,128)(2,1)}), s16[16,4,64,128]{3,2,1,0:T(8,128)(2,1)S(1)}, u32[]{:S(2)}, u32[]{:S(2)}) async-start(s16[16,4,64,128]{3,2,1,0:T(8,128)(2,1)} %all_layers.3), calls=%async_computation.1 | async-start | bytes 2097152 | tf_op jit(solution)/shard_map/all_to_all | solution.py:369
  54.8 3.4 %copy-start = (bf16[16,128,2048]{2,1,0:T(8,128)(2,1)S(1)}, bf16[16,128,2048]{2,1,0:T(8,128)(2,1)}, u32[]{:S(2)}) copy-start(bf16[16,128,2048]{2,1,0:T(8,128)(2,1)} %refs_1_.7) | copy-start | bytes 25165828
  81.7 7.2 %copy-start.1 = (s16[16,4,64,128]{3,2,1,0:T(8,128)(2,1)}, s16[16,4,64,128]{3,2,1,0:T(8,128)(2,1)S(1)}, u32[]{:S(2)}) copy-start(s16[16,4,64,128]{3,2,1,0:T(8,128)(2,1)S(1)} %all-to-all-done.1.got_ref) | copy-start | bytes 3145732
  81.8 23.0 %all-to-all-start = ((s16[16,4,64,128]{3,2,1,0:T(8,128)(2,1)}), s16[16,4,64,128]{3,2,1,0:T(8,128)(2,1)S(1)}, u32[]{:S(2)}, u32[]{:S(2)}) async-start(s16[16,4,64,128]{3,2,1,0:T(8,128)(2,1)} %ends_layers.1), calls=%async_computation | async-start | bytes 2097152 | tf_op jit(solution)/shard_map/all_to_all | solution.py:372
  104.8 1.0 copy-start.2
Sparse Core Ops, SparseCore 0:
  9.1 26.0 all-gather.2

commit v3 on v2

v3 whole, which is shorter than its diff:
```python
import jax
import jax.numpy as jnp
import numpy as np
from jax import lax
from jax.experimental import pallas as pl
from jax.experimental.pallas import tpu as pltpu
from jax.sharding import PartitionSpec as P

LANES = 128
SUBLANES = 8
PIECE = 256
LOAD = 256
f32 = jnp.float32
LANE_LOOKUP = lax.GatherDimensionNumbers(
    offset_dims=(),
    collapsed_slice_dims=(1,),
    start_index_map=(1,),
    operand_batching_dims=(0,),
    start_indices_batching_dims=(0,),
)
KAPPA = -2.0 / float(np.log(2.0))
HIGH_STEPS = 32766.0
LOW_STEPS = 65535.0
CENTRE = 16.0
STEPS = 2340.0
LEAST = 2.0**-29.9


def strip_pipeline(tables, rim_rows, inside, before_ref, after_ref, heat_hbm, entry_hbm, state_ref, out_hbm, out_ref, out_row, diff, heat, entry,
                   ta, da, tb, db, heat_sem, entry_sem, out_sem, *, segments, mode, sight):
    all_rows, columns = heat_hbm.shape[1:]
    layers = heat_hbm.shape[0]
    height = segments[0][1]
    count = columns // PIECE
    strips = PIECE // LANES
    if mode == "all":
        centres, shift, extras = list(range(1, layers + 1)), 1, {0: "before", layers + 1: "after"}
    elif mode == "mid":
        centres, shift, extras = list(range(1, layers - 1)), 0, {0: 0, layers - 1: layers - 1}
    else:
        centres, shift, extras = [1, 4], 1, {0: "before", 2: 1, 3: 2, 5: "after"}
    stride = centres[1] - centres[0]
    parts = strips if height > 16 else 1
    share = len(centres) // parts
    batch = min(share, 128 // height)
    while share % batch:
        batch -= 1
    units_at_once = 4 if height % 32 == 0 else 2

    load = columns if mode == "ends" else LOAD
    loads, each = columns // load, load // PIECE
    ahead = 2 if each == 1 else 1
    adjacent = segments[1][0] == segments[0][0] + height
    blocks_of_rows = [(segments[0][0], 0, 2 * height)] if adjacent else [(row, k * height, height) for k, (row, _) in enumerate(segments)]

    def heat_copies(p):
        cols = pl.ds(pl.multiple_of(p * load, load), load)
        into = pl.ds(pl.multiple_of(2 * LANES + p * load, LANES), load)
        found = []
        for k, (row, _) in enumerate(segments):
            low, high = max(row - 16, 0), min(row + height + 16, all_rows)
            target = pl.ds(16 - (row - low), high - low)
            pairs = [(0, 0, 2), (layers - 2, 2, 2)] if mode == "ends" else [(0, 0, layers)]
            for n, (source, first, size) in enumerate(pairs):
                found.append(
                    pltpu.make_async_copy(
                        heat_hbm.at[pl.ds(source, size), pl.ds(low, high - low), cols],
                        heat.at[k, pl.ds(first, size), target, into],
                        heat_sem.at[2 * k + n, p],
                    )
                )
        return found

    def entry_copies(p):
        cols = pl.ds(pl.multiple_of(p * load, load), load)
        found = []
        for k, (row, own, size) in enumerate(blocks_of_rows):
            if mode == "ends":
                pairs = [(0, 0, 1), (layers - 1, 1, 1)]
            else:
                pairs = [(1 if mode == "mid" else 0, 0, len(centres))]
            for n, (source, first, deep) in enumerate(pairs):
                found.append(
                    pltpu.make_async_copy(
                        entry_hbm.at[pl.ds(source, deep), pl.ds(row, size), cols],
                        entry.at[pl.ds(first, deep), pl.ds(own, size), cols],
                        entry_sem.at[2 * k + n, p],
                    )
                )
        return found

    def out_copy(p):
        here = pl.ds(p * (load // LANES), load // LANES)
        rows = pl.ds(out_row, 2 * height)
        return pltpu.make_async_copy(out_ref.at[here, :, rows], out_hbm.at[here, :, rows], out_sem.at[p])

    def start(copies):
        for copy in copies:
            copy.start()

    def wait(copies):
        for copy in copies:
            copy.wait()

    def begin():
        for p in range(min(ahead, loads)):
            start(heat_copies(p))
        for p in range(loads):
            start(entry_copies(p))
            if p + ahead < loads:
                start(heat_copies(p + ahead))
        heat[:, :, :, 0 : 2 * LANES] = jnp.zeros(heat.shape[:3] + (2 * LANES,), jnp.bfloat16)
        heat[:, :, :, 2 * LANES + columns :] = jnp.zeros(heat.shape[:3] + (LANES,), jnp.bfloat16)

    def prepare(p, seg, t, dv, n, qs):
        row = segments[seg][0]
        own = pl.ds(pl.multiple_of(p * PIECE, PIECE), PIECE)
        cols = pl.ds(pl.multiple_of(2 * LANES + p * PIECE, LANES), PIECE)
        wide = pl.ds(pl.multiple_of(LANES + p * PIECE, LANES), PIECE + 2 * LANES)
        mid = slice(16, 16 + height)

        def put(slot, first, value):
            for q in range(strips):
                t[q, slot, first : first + value.shape[0], :] = value[:, q * LANES : (q + 1) * LANES]

        for q in qs:
            for slot, source in extras.items():
                here = pl.multiple_of(p * PIECE + q * LANES, LANES)
                if source == "before":
                    value = before_ref[row : row + height, pl.ds(here, LANES)].astype(f32) * inside[0]
                elif source == "after":
                    value = after_ref[row : row + height, pl.ds(here, LANES)].astype(f32) * inside[1]
                else:
                    value = heat[seg, source, mid, pl.ds(2 * LANES + here, LANES)].astype(f32)
                t[q, slot, 8 : 8 + height, :] = value
        for first in range(0, share, batch):
            at = n * share + first
            slot0 = centres[0] + stride * at
            if stride == 1:
                window = heat[seg, pl.ds(slot0 - shift, batch), mid, wide].reshape(batch * height, PIECE + 2 * LANES)
            else:
                window = jnp.concatenate([heat[seg, centres[0] - shift + stride * (at + m), mid, wide] for m in range(batch)], axis=0)
            moved = jnp.dot(window, diff[...], preferred_element_type=f32).reshape(batch, height, PIECE)
            for q in range(strips):
                dv[q, pl.ds(at, batch)] = moved[:, :, q * LANES : (q + 1) * LANES]
            for m in range(batch):
                slot = slot0 + stride * m
                z = slot - shift
                layer = z if mode != "ends" else jnp.where(at + m == 0, 0, layers - 1)
                put(slot, 8, heat[seg, z, mid, cols].astype(f32))
                if row == 0:
                    put(slot, 7, rim_rows[0, pl.ds(layer, 1), own])
                else:
                    put(slot, 0, heat[seg, z, 0:16, cols].astype(f32)[8:16])
                if row + height == all_rows:
                    put(slot, 8 + height, rim_rows[1, pl.ds(layer, 1), own])
                else:
                    put(slot, 8 + height, heat[seg, z, 16 + height : 32 + height, cols].astype(f32)[0:8])
                yield

    def looked(index):
        rg, ba = [
            lax.gather(table, index[:, :, None], LANE_LOOKUP, (1, 1), mode=lax.GatherScatterMode.PROMISE_IN_BOUNDS)
            for table in tables
        ]
        return rg.astype(f32), (rg & 0xFFFF).astype(f32), ba.astype(f32), (ba & 0xFFFF).astype(f32) * (4.0 / (sight * LOW_STEPS))

    scale = 0.7 / 9.0
    scales = [scale / (HIGH_STEPS * 65536.0), scale / LOW_STEPS, scale / (HIGH_STEPS * 65536.0)]

    def composite(p, seg, t, dv, qs):
        jobs = [(q, r0) for q in qs for r0 in range(0, height, SUBLANES)]
        size = units_at_once if parts > 1 else len(jobs)
        for group in range(0, len(jobs), size):
            units = []
            for q, r0 in jobs[group : group + size]:
                s = strips * p + q
                units.append(
                    dict(
                        q=q,
                        s=s,
                        r0=r0,
                        cols=pl.ds(pl.multiple_of(s * LANES, LANES), LANES),
                        trans=jnp.ones((SUBLANES, LANES), f32),
                        colors=[jnp.zeros((SUBLANES, LANES), f32) for channel in range(3)],
                        prev=t[q, centres[0] - 1, 8 + r0 : 16 + r0, :],
                        cur=t[q, centres[0], 8 + r0 : 16 + r0, :],
                    )
                )
            for at, slot in enumerate(centres):
                for unit in units:
                    q, r0 = unit["q"], unit["r0"]
                    if mode == "ends" and at == 1:
                        kept = [state_ref[unit["s"], channel, seg * height + r0 : seg * height + r0 + 8, :] for channel in range(4)]
                        unit["colors"] = [old + unit["trans"] * new for old, new in zip(unit["colors"], kept)]
                        unit["trans"] = unit["trans"] * kept[3]
                        unit["prev"], unit["cur"] = t[q, slot - 1, 8 + r0 : 16 + r0, :], t[q, slot, 8 + r0 : 16 + r0, :]
                    nxt = t[q, slot + 1, 8 + r0 : 16 + r0, :]
                    a = nxt - unit["prev"]
                    b = t[q, slot, 9 + r0 : 17 + r0, :] - t[q, slot, 7 + r0 : 15 + r0, :]
                    c = dv[q, at, r0 : r0 + 8, :]
                    m = b + c
                    lit = a + m + m
                    square = (a * a + b * b) + (c * c + 4.0)
                    shade = lit * lit * pl.reciprocal(square, approx=True) + 0.3 / scale
                    red, green, blue, weight = looked(entry[at, seg * height + r0 : seg * height + r0 + 8, unit["cols"]])
                    alpha = weight * pl.reciprocal(jnp.exp2(unit["cur"] * KAPPA) + 1.0, approx=True)
                    part = alpha * unit["trans"]
                    unit["trans"] = unit["trans"] - part
                    shown = shade * part
                    unit["colors"] = [old + new * shown for old, new in zip(unit["colors"], (red, green, blue))]
                    unit["prev"], unit["cur"] = unit["cur"], nxt
                yield
            for pair in range(0, len(units), 2):
                twin = units[pair : pair + 2]
                r0 = out_row + seg * height + twin[0]["r0"]
                for channel in range(4):
                    if mode == "mid":
                        values = [unit["colors"][channel] if channel < 3 else unit["trans"] for unit in twin]
                        out_ref[twin[0]["s"], channel, r0 : r0 + 16, :] = jnp.concatenate(values, axis=0)
                        continue
                    values = [unit["colors"][channel] * scales[channel] if channel < 3 else 1.0 - unit["trans"] for unit in twin]
                    code = jnp.round((jnp.log2(jnp.maximum(jnp.concatenate(values, axis=0), LEAST)) + CENTRE) * STEPS)
                    out_ref[twin[0]["s"], channel, r0 : r0 + 16, :] = code.astype(jnp.int32).astype(jnp.int16)

    def both(first, second):
        def part(n, carry):
            qs = [n] if parts > 1 else list(range(strips))
            following = prepare(*second, n, qs)
            groups = max(height // (SUBLANES * units_at_once), 1) if parts > 1 else 1
            steps = max(groups * len(centres) // share, 1)
            for at, step in enumerate(composite(*first, qs)):
                if at % steps == 0:
                    next(following, None)
            for step in following:
                pass
            return carry

        if parts > 1:
            lax.fori_loop(0, parts, part, 0)
        else:
            part(0, 0)

    def run():
        for p in range(min(ahead, loads)):
            wait(heat_copies(p))
        for n in range(parts):
            for step in prepare(0, 0, ta, da, n, [n] if parts > 1 else list(range(strips))):
                pass

        def body(i, carry):
            @pl.when(i % each == 0)
            def _():
                wait(entry_copies(i // each))

            @pl.when((i % each == 0) & (i // each + ahead < loads))
            def _():
                wait(heat_copies(i // each + ahead))

            both((i, 0, ta, da), (i, 1, tb, db))
            both((i, 1, tb, db), (jnp.minimum(i + 1, count - 1), 0, ta, da))

            @pl.when(i % each == each - 1)
            def _():
                out_copy(i // each).start()

            return carry

        lax.fori_loop(0, count, body, 0)

    def finish():
        for p in range(loads):
            out_copy(p).wait()

    return begin, run, finish


def lookup_words(table_ref, padded):
    padded[...] = jnp.zeros(padded.shape, f32)
    padded[0:4, 0 : table_ref.shape[1]] = table_ref[...]
    tables = []
    for pair in range(2):
        low_half = jnp.round(padded[2 * pair + 1 : 2 * pair + 2, :] * LOW_STEPS)
        high_half = jnp.round(padded[2 * pair : 2 * pair + 1, :] * HIGH_STEPS - low_half * (1.0 / 65536.0))
        words = high_half.astype(jnp.int32) * 65536 + low_half.astype(jnp.int32)
        tables.append(jnp.broadcast_to(words, (SUBLANES, LANES)))
    return tables


def brick(table, heat, entry, groups, sight, before=None, after=None, upper=None, lower=None, state=None):
    layers, all_rows, columns = heat.shape
    pieces = columns // PIECE
    blocks = columns // LANES
    rows_of = [2 * segments[0][1] for segments, mode in groups]
    total = sum(rows_of)
    out_type = f32 if groups[0][1] == "mid" else jnp.int16
    whole = pl.BlockSpec(memory_space=pltpu.HBM)
    inside = pl.BlockSpec(memory_space=pltpu.VMEM)
    given = {"table": (table, whole), "heat": (heat, whole), "entry": (entry, whole)}
    if before is not None:
        given["before"], given["after"] = (before, inside), (after, inside)
    if upper is not None:
        given["upper"], given["lower"] = (upper, inside), (lower, inside)
    if state is not None:
        given["state"] = (state, whole)
    names = list(given)
    common = [
        pltpu.VMEM(table.shape, f32),
        pltpu.VMEM((SUBLANES, LANES), f32),
        pltpu.VMEM((2, layers, columns), f32),
        pltpu.VMEM((PIECE + 2 * LANES, PIECE), jnp.bfloat16),
        pltpu.VMEM((blocks, 4, total, LANES), out_type),
        pltpu.VMEM((blocks, 4, 2 * groups[0][0][0][1] if state is not None else SUBLANES, LANES), f32),
        pltpu.SemaphoreType.DMA,
        pltpu.SemaphoreType.DMA,
    ]
    own = []
    for segments, mode in groups:
        height = segments[0][1]
        held, centres = {"all": (layers, layers), "mid": (layers, layers - 2), "ends": (4, 2)}[mode]
        slots = {"all": layers + 2, "mid": layers, "ends": 6}[mode]
        t = pltpu.VMEM((PIECE // LANES, slots, height + 16, LANES), f32)
        dv = pltpu.VMEM((PIECE // LANES, centres, height, LANES), f32)
        own += [
            pltpu.VMEM((2, held, height + 32, columns + 3 * LANES), jnp.bfloat16),
            pltpu.VMEM((centres, 2 * height, columns), jnp.int32),
            t,
            dv,
            t,
            dv,
            pltpu.SemaphoreType.DMA((4, pieces)),
            pltpu.SemaphoreType.DMA((4, pieces)),
            pltpu.SemaphoreType.DMA((pieces,)),
        ]

    def kernel(*refs):
        ref = dict(zip(names, refs))
        out_hbm = refs[len(names)]
        table_ref, padded, rim_rows, diff, out_ref, state_ref, state_sem, table_sem, *rest = refs[len(names) + 1 :]
        here, side = lax.axis_index("depth"), lax.axis_index("cross")
        flags = [(here > 0).astype(f32), (here < lax.axis_size("depth") - 1).astype(f32)]
        table_copy = pltpu.make_async_copy(ref["table"], table_ref, table_sem)
        table_copy.start()
        tables = []
        if state is not None:
            state_copy = pltpu.make_async_copy(ref["state"], state_ref, state_sem)
            state_copy.start()
        runs, row = [], 0
        for n, (segments, mode) in enumerate(groups):
            runs.append(
                strip_pipeline(tables, rim_rows, flags, ref.get("before"), ref.get("after"), ref["heat"], ref["entry"], state_ref,
                               out_hbm, out_ref, row, diff, *rest[9 * n : 9 * n + 9], segments=segments, mode=mode, sight=sight)
            )
            row += rows_of[n]
        for begin, run, finish in runs:
            begin()
        table_copy.wait()
        tables += lookup_words(table_ref, padded)
        k = lax.broadcasted_iota(jnp.int32, diff.shape, 0) - lax.broadcasted_iota(jnp.int32, diff.shape, 1)
        diff[...] = jnp.where(k == LANES + 1, 1.0, jnp.where(k == LANES - 1, -1.0, 0.0)).astype(jnp.bfloat16)
        if upper is not None:
            rim_rows[0] = ref["upper"][...].astype(f32) * (side > 0).astype(f32)
            rim_rows[1] = ref["lower"][...].astype(f32) * (side < lax.axis_size("cross") - 1).astype(f32)
        if state is not None:
            state_copy.wait()
        for begin, run, finish in runs:
            run()
        for begin, run, finish in runs:
            finish()

    return pl.pallas_call(
        kernel,
        in_specs=[given[name][1] for name in names],
        out_specs=whole,
        out_shape=jax.ShapeDtypeStruct((blocks, 4, total, LANES), out_type),
        scratch_shapes=common + own,
        compiler_params=pltpu.CompilerParams(vmem_limit_bytes=36 * 1024 * 1024),
        name="_".join(mode for segments, mode in groups) + "_layers",
    )(*[given[name][0] for name in names])


def merge_kernel(got, *rest, places):
    out_hbm, image, image_sem = rest[-3:]
    count, channels, rows, lanes = got.shape

    def image_copy(k):
        return pltpu.make_async_copy(image.at[k], out_hbm.at[:, pl.ds(16 * places[k], 16)], image_sem.at[k])

    for k in range(len(places)):
        colors = [jnp.zeros((16, lanes), f32) for channel in range(3)]
        trans = jnp.ones((16, lanes), f32)
        for source in range(count):
            value = [
                jnp.exp2(got[source, channel, 16 * k : 16 * k + 16].astype(f32) * (1.0 / STEPS) - CENTRE)
                for channel in range(4)
            ]
            colors = [old + trans * new for old, new in zip(colors, value)]
            trans = trans - trans * value[3]
        for channel in range(4):
            image[k, channel] = colors[channel] if channel < 3 else 1.0 - trans
        image_copy(k).start()
    for k in range(len(places)):
        image_copy(k).wait()


def merge(got, image, all_rows, places):
    count, channels, rows, lanes = got.shape
    whole = pl.BlockSpec(memory_space=pltpu.HBM)
    operands = [got] if image is None else [got, image]

    def kernel(*refs):
        merge_kernel(*refs, places=places)

    return pl.pallas_call(
        kernel,
        in_specs=[pl.BlockSpec(memory_space=pltpu.VMEM), whole][: len(operands)],
        out_specs=whole,
        out_shape=jax.ShapeDtypeStruct((channels, all_rows, lanes), f32),
        scratch_shapes=[
            pltpu.VMEM((len(places), channels, 16, lanes), f32),
            pltpu.SemaphoreType.DMA((len(places),)),
        ],
        input_output_aliases={} if image is None else {1: 0},
        compiler_params=pltpu.CompilerParams(vmem_limit_bytes=16 * 1024 * 1024),
        name="merge",
    )(*operands)


def local(heat, entry, table):
    count = lax.axis_size("depth")
    sides = lax.axis_size("cross")
    layers, rows, columns = heat.shape
    sight = layers * count

    def turned(value, axis, by):
        size = lax.axis_size(axis)
        return lax.ppermute(value, axis, [(i, (i + by) % size) for i in range(size)])

    before = turned(heat[-1], "depth", 1)
    after = turned(heat[0], "depth", -1)
    upper = turned(heat[:, -1, :], "cross", 1)
    lower = turned(heat[:, 0, :], "cross", -1)

    heat = pltpu.with_memory_space_constraint(heat, pltpu.HBM)
    entry = pltpu.with_memory_space_constraint(entry, pltpu.HBM)
    table = pltpu.with_memory_space_constraint(table, pltpu.HBM)
    centre, inner, outer = ((48, 16), (64, 16)), ((32, 16), (80, 16)), ((0, 32), (96, 32))
    state = brick(table, heat, entry, [(centre, "mid")], sight)
    codes = brick(table, heat, entry, [(centre, "ends"), (inner, "all")], sight, before=before, after=after, upper=upper, lower=lower, state=state)
    codes, before = lax.optimization_barrier((codes, before))
    first = lax.all_to_all(codes, "depth", 0, 0, tiled=True)
    codes = brick(table, heat, entry, [(outer, "all")], sight, before=before, after=after, upper=upper, lower=lower)
    second = lax.all_to_all(codes, "depth", 0, 0, tiled=True)
    image = merge(first, None, rows, (3, 4, 2, 5))
    return merge(second, image, rows, (0, 1, 6, 7))


def solution(mesh):
    in_specs = (P("depth", "cross", None), P("depth", "cross", None), P())
    out_specs = P(None, "cross", "depth")
    return jax.shard_map(local, mesh=mesh, in_specs=in_specs, out_specs=out_specs, check_vma=False)
```

time: 117 us -> 83.4 us (0.71)
  between operations: 13.5 us -> 0.12 us
  waiting for transfers between devices: 22.4 us -> 17.3 us
  local copies, waits for them, and re-layouts: 7.81 us -> 2.79 us
  Pallas kernels: 47.5 us -> 42.8 us
  starting transfers between devices: 23.2 us -> 20.1 us
  other arithmetic: 1.58 us -> 0 us
    ppermute x2 -> x4, waiting for transfers between devices: 10 us -> 2.21 us  [turned(): lax.ppermute(value, axis, [(i, (i + by) % size) for i in range(size)])]
    all_to_all x1, starting transfers between devices: 10.1 us -> 4.31 us  [local(): first = lax.all_to_all(codes, 'depth', 0, 0, tiled=True)]
    pallas_call x6 -> x5, Pallas kernels: 47.5 us -> 42.8 us  [the longest x3 40.5 us: brick(): pl.pallas_call(kernel, in_specs=[given[name][1] for name in names], out_s...]
    unnamed x6 -> x2, local copies, waits for them, and re-layouts: 4.36 us -> 0.09 us
    all_to_all x1, waiting for transfers between devices: 12.4 us -> 15.1 us  [local(): second = lax.all_to_all(codes, 'depth', 0, 0, tiled=True)]
    ppermute x2 -> x4, starting transfers between devices: 5.87 us -> 8.59 us  [turned(): lax.ppermute(value, axis, [(i, (i + by) % size) for i in range(size)])]
  transfers between devices with their start and end apart: 5 -> 6, of which waited for: 3 -> 2; matrix products, arithmetic and copies ran while one was open for 2% -> 2% of each run, Pallas kernels for 38% -> 34%
where the time goes in v3:
time: 83.4 us; the launch traced here: 83.1 us
  Pallas kernels  42.8 us (51%)
  starting transfers between devices  20.1 us (24%)
  waiting for transfers between devices  17.3 us (21%)
  local copies, waits for them, and re-layouts  2.79 us (3%)
    pallas_call x3, Pallas kernels, brick(): pl.pallas_call(kernel, in_specs=[given[name][1] for name in names], out_s...  40.5 us
    all_to_all x1, waiting for transfers between devices, local(): second = lax.all_to_all(codes, 'depth', 0, 0, tiled=True)  15.1 us
    ppermute x4, starting transfers between devices, turned(): lax.ppermute(value, axis, [(i, (i + by) % size) for i in range(size)])  8.59 us
    all_to_all x1, starting transfers between devices, local(): second = lax.all_to_all(codes, 'depth', 0, 0, tiled=True)  7.22 us
    all_to_all x1, starting transfers between devices, local(): first = lax.all_to_all(codes, 'depth', 0, 0, tiled=True)  4.31 us
    pallas_call x2, Pallas kernels, merge(): pl.pallas_call(kernel, in_specs=[pl.BlockSpec(memory_space=pltpu.VMEM), w...  2.25 us
    ppermute x4, waiting for transfers between devices, turned(): lax.ppermute(value, axis, [(i, (i + by) % size) for i in range(size)])  2.21 us
  transfers between devices with their start and end apart: 6, of which 2 were waited for; matrix products, arithmetic and copies ran while one was open for 2% of the time, Pallas kernels for 34%

profile of v3, /device:TPU:0, one launch (start us, length us, event | category | flops | bytes accessed | tf_op | source)
XLA Modules:
  0.0 83.1 jit_solution(11809113284846341348)
XLA Ops:
  0.0 1.3 %slice_bitcast_fusion = (bf16[128,2048]{1,0:T(8,128)(2,1)S(1)}, bf16[128,2048]{1,0:T(8,128)(2,1)S(1)}) fusion(bf16[16,128,2048]{2,1,0:T(8,128)(2,1)} %refs_1_.5), kind=kLoop, calls=%fused_computation | loop fusion | bytes 2097152 | tf_op jit(solution)/shard_map/squeeze | solution.py:440
  1.3 5.4 %collective-permute-start.1 = (bf16[128,2048]{1,0:T(8,128)(2,1)S(1)}, bf16[128,2048]{1,0:T(8,128)(2,1)S(1)}, u32[]{:S(2)}, u32[]{:S(2)}) collective-permute-start(bf16[128,2048]{1,0:T(8,128)(2,1)S(1)} %get-tuple-element.11), channel_id=1, source_target_pairs={{0,120},{8,0},{16,8},{24,16},{32,24},{40,32},{48,40},{56,48},{64,5... | collective-permute-start | bytes 1572872 | tf_op jit(solution)/shard_map/ppermute | solution.py:437
  6.7 0.0 collective-permute-start
  6.7 1.4 %fusion = (bf16[16,1,2048]{2,1,0:T(2,128)(2,1)S(1)}, bf16[16,1,2048]{2,1,0:T(2,128)(2,1)S(1)}) fusion(bf16[16,128,2048]{2,1,0:T(8,128)(2,1)} %refs_1_.5), kind=kLoop, calls=%fused_computation.4 | loop fusion | bytes 262144 | tf_op jit(solution)/shard_map/slice | solution.py:442
  8.1 0.0 collective-permute-start.2
  8.2 3.2 %collective-permute-start.3 = (bf16[16,2048]{1,0:T(8,128)(2,1)S(1)}, bf16[16,2048]{1,0:T(8,128)(2,1)S(1)}, u32[]{:S(2)}, u32[]{:S(2)}) collective-permute-start(bf16[16,2048]{1,0:T(8,128)(2,1)S(1)} %bitcast.11), channel_id=1, source_target_pairs={{0,7},{1,0},{2,1},{3,2},{4,3},{5,4},{6,5},{7,6},{8,15},{9,8},{10,9... | collective-permute-start | bytes 196616 | tf_op jit(solution)/shard_map/ppermute | solution.py:437
  11.4 9.7 %mid_layers.1.refs_7_ = f32[16,4,32,128]{3,2,1,0:T(8,128)S(1)} custom-call(f32[4,16]{1,0:T(4,128)} %refs_0_.5, bf16[16,128,2048]{2,1,0:T(8,128)(2,1)} %refs_1_.5, s32[16,128,2048]{2,1,0:T(8,128)} %refs_2_.5), custom_call_target="tpu_custom_call" | custom-call | tf_op jit(solution)/shard_map/mid_layers/pallas_call | solution.py:371
  21.1 0.0 collective-permute-done.2.refs_5_
  21.2 0.0 collective-permute-done.3.refs_6_
  21.2 0.0 collective-permute-done.1.refs_4_
  21.2 2.2 %collective-permute-done.refs_3_ = bf16[128,2048]{1,0:T(8,128)(2,1)S(1)} collective-permute-done((bf16[128,2048]{1,0:T(8,128)(2,1)S(1)}, bf16[128,2048]{1,0:T(8,128)(2,1)S(1)}, u32[]{:S(2)}, u32[]{:S(2)}) %collective-permute-start) | collective-permute-done | bytes 524320 | tf_op jit(solution)/shard_map/ppermute | solution.py:437
  23.4 13.1 %ends_all_layers.1 = s16[16,4,64,128]{3,2,1,0:T(8,128)(2,1)} custom-call(f32[4,16]{1,0:T(4,128)} %refs_0_.5, bf16[16,128,2048]{2,1,0:T(8,128)(2,1)} %refs_1_.5, s32[16,128,2048]{2,1,0:T(8,128)} %refs_2_.5, bf16[128,2048]{1,0:T(8,128)(2,1)S(1)} %collective-permute-done.refs_3_, bf16[128,2048]{1,0:T(8,128)(2,1)S(1)} %collective-permute-done.1.refs_4_, ...), custom_call_target="tpu_custom_call" | custom-call | tf_op jit(solution)/shard_map/ends_all_layers/pallas_call | solution.py:371
  36.5 4.3 %all-to-all-start.1 = ((s16[16,4,64,128]{3,2,1,0:T(8,128)(2,1)}), s16[16,4,64,128]{3,2,1,0:T(8,128)(2,1)S(1)}, u32[]{:S(2)}, u32[]{:S(2)}) async-start(s16[16,4,64,128]{3,2,1,0:T(8,128)(2,1)} %ends_all_layers.1), calls=%async_computation.1 | async-start | bytes 2097152 | tf_op jit(solution)/shard_map/all_to_all | solution.py:451
  40.8 17.7 %all_layers.1 = s16[16,4,64,128]{3,2,1,0:T(8,128)(2,1)} custom-call(f32[4,16]{1,0:T(4,128)} %refs_0_.5, bf16[16,128,2048]{2,1,0:T(8,128)(2,1)} %refs_1_.5, s32[16,128,2048]{2,1,0:T(8,128)} %refs_2_.5, bf16[128,2048]{1,0:T(8,128)(2,1)S(1)} %collective-permute-done.refs_3_, bf16[128,2048]{1,0:T(8,128)(2,1)S(1)} %collective-permute-done.1.refs_4_, ...), custom_call_target="tpu_custom_call" | custom-call | tf_op jit(solution)/shard_map/all_layers/pallas_call | solution.py:371
  58.5 0.0 all-to-all-done.1.refs_0_
  58.5 7.2 %all-to-all-start = ((s16[16,4,64,128]{3,2,1,0:T(8,128)(2,1)}), s16[16,4,64,128]{3,2,1,0:T(8,128)(2,1)S(1)}, u32[]{:S(2)}, u32[]{:S(2)}) async-start(s16[16,4,64,128]{3,2,1,0:T(8,128)(2,1)} %all_layers.1), calls=%async_computation | async-start | bytes 2097152 | tf_op jit(solution)/shard_map/all_to_all | solution.py:453
  65.7 1.1 %merge.2.refs_1_ = f32[4,128,128]{2,1,0:T(8,128)} custom-call(s16[16,4,64,128]{3,2,1,0:T(8,128)(2,1)S(1)} %all-to-all-done.1.refs_0_), custom_call_target="tpu_custom_call" | custom-call | tf_op jit(solution)/shard_map/merge/pallas_call | solution.py:414
  66.9 15.1 %all-to-all-done.refs_0_ = s16[16,4,64,128]{3,2,1,0:T(8,128)(2,1)S(1)} async-done(((s16[16,4,64,128]{3,2,1,0:T(8,128)(2,1)}), s16[16,4,64,128]{3,2,1,0:T(8,128)(2,1)S(1)}, u32[]{:S(2)}, u32[]{:S(2)}) %all-to-all-start) | async-done | bytes 1048608 | tf_op jit(solution)/shard_map/all_to_all | solution.py:453
  82.0 1.1 %merge.3 = f32[4,128,128]{2,1,0:T(8,128)} custom-call(s16[16,4,64,128]{3,2,1,0:T(8,128)(2,1)S(1)} %all-to-all-done.refs_0_, f32[4,128,128]{2,1,0:T(8,128)} %merge.2.refs_1_), custom_call_target="tpu_custom_call", output_to_operand_aliasing={{}: (1, {})} | custom-call | tf_op jit(solution)/shard_map/merge/pallas_call | solution.py:414
  (2 shorter events, 0.1 us)
Async XLA Ops:
  1.3 19.9 %collective-permute-start.1 = (bf16[128,2048]{1,0:T(8,128)(2,1)S(1)}, bf16[128,2048]{1,0:T(8,128)(2,1)S(1)}, u32[]{:S(2)}, u32[]{:S(2)}) collective-permute-start(bf16[128,2048]{1,0:T(8,128)(2,1)S(1)} %get-tuple-element.11), channel_id=1, source_target_pairs={{0,120},{8,0},{16,8},{24,16},{32,24},{40,32},{48,40},{56,48},{64,5... | collective-permute-start | bytes 1572872 | tf_op jit(solution)/shard_map/ppermute | solution.py:437
  6.7 16.7 %collective-permute-start = (bf16[128,2048]{1,0:T(8,128)(2,1)S(1)}, bf16[128,2048]{1,0:T(8,128)(2,1)S(1)}, u32[]{:S(2)}, u32[]{:S(2)}) collective-permute-start(bf16[128,2048]{1,0:T(8,128)(2,1)S(1)} %get-tuple-element.12), channel_id=1, source_target_pairs={{0,8},{8,16},{16,24},{24,32},{32,40},{40,48},{48,56},{56,64},{64,7... | collective-permute-start | bytes 1572872 | tf_op jit(solution)/shard_map/ppermute | solution.py:437
  8.1 13.0 %collective-permute-start.2 = (bf16[16,2048]{1,0:T(8,128)(2,1)S(1)}, bf16[16,2048]{1,0:T(8,128)(2,1)S(1)}, u32[]{:S(2)}, u32[]{:S(2)}) collective-permute-start(bf16[16,2048]{1,0:T(8,128)(2,1)S(1)} %bitcast.10), channel_id=1, source_target_pairs={{0,1},{1,2},{2,3},{3,4},{4,5},{5,6},{6,7},{7,0},{8,9},{9,10},{10,1... | collective-permute-start | bytes 196616 | tf_op jit(solution)/shard_map/ppermute | solution.py:437
  8.2 12.9 %collective-permute-start.3 = (bf16[16,2048]{1,0:T(8,128)(2,1)S(1)}, bf16[16,2048]{1,0:T(8,128)(2,1)S(1)}, u32[]{:S(2)}, u32[]{:S(2)}) collective-permute-start(bf16[16,2048]{1,0:T(8,128)(2,1)S(1)} %bitcast.11), channel_id=1, source_target_pairs={{0,7},{1,0},{2,1},{3,2},{4,3},{5,4},{6,5},{7,6},{8,15},{9,8},{10,9... | collective-permute-start | bytes 196616 | tf_op jit(solution)/shard_map/ppermute | solution.py:437
  36.5 22.0 %all-to-all-start.1 = ((s16[16,4,64,128]{3,2,1,0:T(8,128)(2,1)}), s16[16,4,64,128]{3,2,1,0:T(8,128)(2,1)S(1)}, u32[]{:S(2)}, u32[]{:S(2)}) async-start(s16[16,4,64,128]{3,2,1,0:T(8,128)(2,1)} %ends_all_layers.1), calls=%async_computation.1 | async-start | bytes 2097152 | tf_op jit(solution)/shard_map/all_to_all | solution.py:451
  58.5 23.5 %all-to-all-start = ((s16[16,4,64,128]{3,2,1,0:T(8,128)(2,1)}), s16[16,4,64,128]{3,2,1,0:T(8,128)(2,1)S(1)}, u32[]{:S(2)}, u32[]{:S(2)}) async-start(s16[16,4,64,128]{3,2,1,0:T(8,128)(2,1)} %all_layers.1), calls=%async_computation | async-start | bytes 2097152 | tf_op jit(solution)/shard_map/all_to_all | solution.py:453

commit v4 on v3

--- a/solution.py
+++ b/solution.py
@@ -10,6 +10,8 @@
 SUBLANES = 8
 PIECE = 256
 LOAD = 256
+SPLIT = 32
+TOGETHER = 8
 f32 = jnp.float32
 LANE_LOOKUP = lax.GatherDimensionNumbers(
     offset_dims=(),
@@ -26,26 +28,21 @@
 LEAST = 2.0**-29.9
 
 
-def strip_pipeline(tables, rim_rows, inside, before_ref, after_ref, heat_hbm, entry_hbm, state_ref, out_hbm, out_ref, out_row, diff, heat, entry,
-                   ta, da, tb, db, heat_sem, entry_sem, out_sem, *, segments, mode, sight):
+def strip_pipeline(tables, rim_rows, inside, before_ref, after_ref, heat_hbm, entry_hbm, state_ref, out_hbm, out_ref, out_row, weights, heat, entry,
+                   rows_by, first_set, second_set, heat_sem, entry_sem, out_sem, *, segments, mode, sight):
     all_rows, columns = heat_hbm.shape[1:]
     layers = heat_hbm.shape[0]
     height = segments[0][1]
     count = columns // PIECE
     strips = PIECE // LANES
-    if mode == "all":
-        centres, shift, extras = list(range(1, layers + 1)), 1, {0: "before", layers + 1: "after"}
-    elif mode == "mid":
-        centres, shift, extras = list(range(1, layers - 1)), 0, {0: 0, layers - 1: layers - 1}
-    else:
-        centres, shift, extras = [1, 4], 1, {0: "before", 2: 1, 3: 2, 5: "after"}
+    centres = {"all": list(range(1, layers + 1)), "mid": list(range(1, layers - 1)), "ends": [1, 4]}[mode]
+    shift = 0 if mode == "mid" else 1
     stride = centres[1] - centres[0]
-    parts = strips if height > 16 else 1
+    parts = strips if height > SPLIT else 1
     share = len(centres) // parts
     batch = min(share, 128 // height)
-    while share % batch:
+    while share % batch or (stride > 1 and batch > 1):
         batch -= 1
-    units_at_once = 4 if height % 32 == 0 else 2
 
     load = columns if mode == "ends" else LOAD
     loads, each = columns // load, load // PIECE
@@ -111,51 +108,32 @@
                 start(heat_copies(p + ahead))
         heat[:, :, :, 0 : 2 * LANES] = jnp.zeros(heat.shape[:3] + (2 * LANES,), jnp.bfloat16)
         heat[:, :, :, 2 * LANES + columns :] = jnp.zeros(heat.shape[:3] + (LANES,), jnp.bfloat16)
-
-    def prepare(p, seg, t, dv, n, qs):
-        row = segments[seg][0]
-        own = pl.ds(pl.multiple_of(p * PIECE, PIECE), PIECE)
+        k = lax.broadcasted_iota(jnp.int32, rows_by.shape, 1) - lax.broadcasted_iota(jnp.int32, rows_by.shape, 0)
+        rows_by[...] = jnp.where(k == 17, 1.0, jnp.where(k == 15, -1.0, 0.0)).astype(jnp.bfloat16)
+        across = slice(2 * LANES, 2 * LANES + columns)
+        for seg, (row, _) in enumerate(segments):
+            for side, at_edge, first in ((0, row == 0, 0), (1, row + height == all_rows, 16 + height)):
+                if at_edge:
+                    for z in range(layers):
+                        rim = jnp.broadcast_to(rim_rows[side, z : z + 1, :], (16, columns))
+                        heat[seg, z, first : first + 16, across] = rim.astype(jnp.bfloat16)
+
+    def prepare(p, seg, kept, n):
         cols = pl.ds(pl.multiple_of(2 * LANES + p * PIECE, LANES), PIECE)
         wide = pl.ds(pl.multiple_of(LANES + p * PIECE, LANES), PIECE + 2 * LANES)
         mid = slice(16, 16 + height)
-
-        def put(slot, first, value):
-            for q in range(strips):
-                t[q, slot, first : first + value.shape[0], :] = value[:, q * LANES : (q + 1) * LANES]
-
-        for q in qs:
-            for slot, source in extras.items():
-                here = pl.multiple_of(p * PIECE + q * LANES, LANES)
-                if source == "before":
-                    value = before_ref[row : row + height, pl.ds(here, LANES)].astype(f32) * inside[0]
-                elif source == "after":
-                    value = after_ref[row : row + height, pl.ds(here, LANES)].astype(f32) * inside[1]
-                else:
-                    value = heat[seg, source, mid, pl.ds(2 * LANES + here, LANES)].astype(f32)
-                t[q, slot, 8 : 8 + height, :] = value
         for first in range(0, share, batch):
             at = n * share + first
-            slot0 = centres[0] + stride * at
-            if stride == 1:
-                window = heat[seg, pl.ds(slot0 - shift, batch), mid, wide].reshape(batch * height, PIECE + 2 * LANES)
-            else:
-                window = jnp.concatenate([heat[seg, centres[0] - shift + stride * (at + m), mid, wide] for m in range(batch)], axis=0)
-            moved = jnp.dot(window, diff[...], preferred_element_type=f32).reshape(batch, height, PIECE)
+            own = centres[0] - shift + stride * at
+            window = heat[seg, pl.ds(own, batch), mid, wide].reshape(batch * height, PIECE + 2 * LANES)
+            moved = jnp.dot(window, weights[...], preferred_element_type=f32).reshape(batch, height, PIECE)
             for q in range(strips):
-                dv[q, pl.ds(at, batch)] = moved[:, :, q * LANES : (q + 1) * LANES]
+                kept[1][q, pl.ds(at, batch)] = moved[:, :, q * LANES : (q + 1) * LANES]
+            yield
             for m in range(batch):
-                slot = slot0 + stride * m
-                z = slot - shift
-                layer = z if mode != "ends" else jnp.where(at + m == 0, 0, layers - 1)
-                put(slot, 8, heat[seg, z, mid, cols].astype(f32))
-                if row == 0:
-                    put(slot, 7, rim_rows[0, pl.ds(layer, 1), own])
-                else:
-                    put(slot, 0, heat[seg, z, 0:16, cols].astype(f32)[8:16])
-                if row + height == all_rows:
-                    put(slot, 8 + height, rim_rows[1, pl.ds(layer, 1), own])
-                else:
-                    put(slot, 8 + height, heat[seg, z, 16 + height : 32 + height, cols].astype(f32)[0:8])
+                moved = jnp.dot(rows_by[...], heat[seg, own + m, :, cols], preferred_element_type=f32)
+                for q in range(strips):
+                    kept[0][q, at + m] = moved[:, q * LANES : (q + 1) * LANES]
                 yield
 
     def looked(index):
@@ -168,9 +146,9 @@
     scale = 0.7 / 9.0
     scales = [scale / (HIGH_STEPS * 65536.0), scale / LOW_STEPS, scale / (HIGH_STEPS * 65536.0)]
 
-    def composite(p, seg, t, dv, qs):
+    def composite(p, seg, kept, qs):
         jobs = [(q, r0) for q in qs for r0 in range(0, height, SUBLANES)]
-        size = units_at_once if parts > 1 else len(jobs)
+        size = min(TOGETHER, len(jobs))
         for group in range(0, len(jobs), size):
             units = []
             for q, r0 in jobs[group : group + size]:
@@ -183,33 +161,46 @@
                         cols=pl.ds(pl.multiple_of(s * LANES, LANES), LANES),
                         trans=jnp.ones((SUBLANES, LANES), f32),
                         colors=[jnp.zeros((SUBLANES, LANES), f32) for channel in range(3)],
-                        prev=t[q, centres[0] - 1, 8 + r0 : 16 + r0, :],
-                        cur=t[q, centres[0], 8 + r0 : 16 + r0, :],
                     )
                 )
+            def layer(slot, unit):
+                r0 = unit["r0"]
+                rows = pl.ds(segments[seg][0] + r0, 16)
+                if slot == 0 and shift:
+                    return before_ref[rows, unit["cols"]].astype(f32) * inside[0]
+                if slot == centres[-1] + 1 and shift:
+                    return after_ref[rows, unit["cols"]].astype(f32) * inside[1]
+                lanes = pl.ds(pl.multiple_of((unit["s"] + 2) * LANES, LANES), LANES)
+                return heat[seg, slot - shift, 16 + r0 : 32 + r0, lanes].astype(f32)
+
             for at, slot in enumerate(centres):
-                for unit in units:
+                for number, unit in enumerate(units):
                     q, r0 = unit["q"], unit["r0"]
+                    if number % 2 == 0:
+                        if at == 0 or stride > 1:
+                            prev, cur = layer(slot - 1, unit), layer(slot, unit)
+                        else:
+                            prev, cur = unit["layers"]
+                        nxt = layer(slot + 1, unit)
+                        unit["layers"] = cur, nxt
+                        steps = nxt - prev
+                    half = slice(0, 8) if number % 2 == 0 else slice(8, 16)
                     if mode == "ends" and at == 1:
-                        kept = [state_ref[unit["s"], channel, seg * height + r0 : seg * height + r0 + 8, :] for channel in range(4)]
-                        unit["colors"] = [old + unit["trans"] * new for old, new in zip(unit["colors"], kept)]
-                        unit["trans"] = unit["trans"] * kept[3]
-                        unit["prev"], unit["cur"] = t[q, slot - 1, 8 + r0 : 16 + r0, :], t[q, slot, 8 + r0 : 16 + r0, :]
-                    nxt = t[q, slot + 1, 8 + r0 : 16 + r0, :]
-                    a = nxt - unit["prev"]
-                    b = t[q, slot, 9 + r0 : 17 + r0, :] - t[q, slot, 7 + r0 : 15 + r0, :]
-                    c = dv[q, at, r0 : r0 + 8, :]
+                        old = [state_ref[unit["s"], channel, seg * height + r0 : seg * height + r0 + 8, :] for channel in range(4)]
+                        unit["colors"] = [held + unit["trans"] * new for held, new in zip(unit["colors"], old)]
+                        unit["trans"] = unit["trans"] * old[3]
+                    a = steps[half]
+                    b, c = [values[q, at, r0 : r0 + 8, :] for values in kept]
                     m = b + c
                     lit = a + m + m
                     square = (a * a + b * b) + (c * c + 4.0)
                     shade = lit * lit * pl.reciprocal(square, approx=True) + 0.3 / scale
                     red, green, blue, weight = looked(entry[at, seg * height + r0 : seg * height + r0 + 8, unit["cols"]])
-                    alpha = weight * pl.reciprocal(jnp.exp2(unit["cur"] * KAPPA) + 1.0, approx=True)
+                    alpha = weight * pl.reciprocal(jnp.exp2(cur[half] * KAPPA) + 1.0, approx=True)
                     part = alpha * unit["trans"]
                     unit["trans"] = unit["trans"] - part
                     shown = shade * part
                     unit["colors"] = [old + new * shown for old, new in zip(unit["colors"], (red, green, blue))]
-                    unit["prev"], unit["cur"] = unit["cur"], nxt
                 yield
             for pair in range(0, len(units), 2):
                 twin = units[pair : pair + 2]
@@ -226,9 +217,9 @@
     def both(first, second):
         def part(n, carry):
             qs = [n] if parts > 1 else list(range(strips))
-            following = prepare(*second, n, qs)
-            groups = max(height // (SUBLANES * units_at_once), 1) if parts > 1 else 1
-            steps = max(groups * len(centres) // share, 1)
+            following = prepare(*second, n)
+            groups = max(len(qs) * height // (SUBLANES * TOGETHER), 1)
+            steps = max(groups * len(centres) // (share // batch * (batch + 1)), 1)
             for at, step in enumerate(composite(*first, qs)):
                 if at % steps == 0:
                     next(following, None)
@@ -245,7 +236,7 @@
         for p in range(min(ahead, loads)):
             wait(heat_copies(p))
         for n in range(parts):
-            for step in prepare(0, 0, ta, da, n, [n] if parts > 1 else list(range(strips))):
+            for step in prepare(0, 0, first_set, n):
                 pass
 
         def body(i, carry):
@@ -257,8 +248,8 @@
             def _():
                 wait(heat_copies(i // each + ahead))
 
-            both((i, 0, ta, da), (i, 1, tb, db))
-            both((i, 1, tb, db), (jnp.minimum(i + 1, count - 1), 0, ta, da))
+            both((i, 0, first_set), (i, 1, second_set))
+            both((i, 1, second_set), (jnp.minimum(i + 1, count - 1), 0, first_set))
 
             @pl.when(i % each == each - 1)
             def _():
@@ -318,16 +309,13 @@
     for segments, mode in groups:
         height = segments[0][1]
         held, centres = {"all": (layers, layers), "mid": (layers, layers - 2), "ends": (4, 2)}[mode]
-        slots = {"all": layers + 2, "mid": layers, "ends": 6}[mode]
-        t = pltpu.VMEM((PIECE // LANES, slots, height + 16, LANES), f32)
-        dv = pltpu.VMEM((PIECE // LANES, centres, height, LANES), f32)
+        kept = [pltpu.VMEM((PIECE // LANES, centres, height, LANES), f32) for number in range(2)]
         own += [
             pltpu.VMEM((2, held, height + 32, columns + 3 * LANES), jnp.bfloat16),
             pltpu.VMEM((centres, 2 * height, columns), jnp.int32),
-            t,
-            dv,
-            t,
-            dv,
+            pltpu.VMEM((height, height + 32), jnp.bfloat16),
+            kept,
+            kept,
             pltpu.SemaphoreType.DMA((4, pieces)),
             pltpu.SemaphoreType.DMA((4, pieces)),
             pltpu.SemaphoreType.DMA((pieces,)),
@@ -336,7 +324,7 @@
     def kernel(*refs):
         ref = dict(zip(names, refs))
         out_hbm = refs[len(names)]
-        table_ref, padded, rim_rows, diff, out_ref, state_ref, state_sem, table_sem, *rest = refs[len(names) + 1 :]
+        table_ref, padded, rim_rows, weights, out_ref, state_ref, state_sem, table_sem, *rest = refs[len(names) + 1 :]
         here, side = lax.axis_index("depth"), lax.axis_index("cross")
         flags = [(here > 0).astype(f32), (here < lax.axis_size("depth") - 1).astype(f32)]
         table_copy = pltpu.make_async_copy(ref["table"], table_ref, table_sem)
@@ -349,18 +337,18 @@
         for n, (segments, mode) in enumerate(groups):
             runs.append(
                 strip_pipeline(tables, rim_rows, flags, ref.get("before"), ref.get("after"), ref["heat"], ref["entry"], state_ref,
-                               out_hbm, out_ref, row, diff, *rest[9 * n : 9 * n + 9], segments=segments, mode=mode, sight=sight)
+                               out_hbm, out_ref, row, weights, *rest[8 * n : 8 * n + 8], segments=segments, mode=mode, sight=sight)
             )
             row += rows_of[n]
-        for begin, run, finish in runs:
-            begin()
-        table_copy.wait()
-        tables += lookup_words(table_ref, padded)
-        k = lax.broadcasted_iota(jnp.int32, diff.shape, 0) - lax.broadcasted_iota(jnp.int32, diff.shape, 1)
-        diff[...] = jnp.where(k == LANES + 1, 1.0, jnp.where(k == LANES - 1, -1.0, 0.0)).astype(jnp.bfloat16)
         if upper is not None:
             rim_rows[0] = ref["upper"][...].astype(f32) * (side > 0).astype(f32)
             rim_rows[1] = ref["lower"][...].astype(f32) * (side < lax.axis_size("cross") - 1).astype(f32)
+        for begin, run, finish in runs:
+            begin()
+        k = lax.broadcasted_iota(jnp.int32, weights.shape, 0) - lax.broadcasted_iota(jnp.int32, weights.shape, 1)
+        weights[...] = jnp.where(k == LANES + 1, 1.0, jnp.where(k == LANES - 1, -1.0, 0.0)).astype(jnp.bfloat16)
+        table_copy.wait()
+        tables += lookup_words(table_ref, padded)
         if state is not None:
             state_copy.wait()
         for begin, run, finish in runs:

time: 83.4 us -> 81.9 us (0.982)
  Pallas kernels: 42.8 us -> 41.2 us
    pallas_call x3, Pallas kernels: 40.5 us -> 38.9 us  [brick(): pl.pallas_call(kernel, in_specs=[given[name][1] for name in names], out_s...]
where the time goes in v4:
time: 81.9 us; the launch traced here: 81.5 us
  Pallas kernels  41.2 us (50%)
  starting transfers between devices  19.9 us (24%)
  waiting for transfers between devices  17.6 us (21%)
  local copies, waits for them, and re-layouts  2.79 us (3%)
    pallas_call x3, Pallas kernels, brick(): pl.pallas_call(kernel, in_specs=[given[name][1] for name in names], out_s...  38.9 us
    all_to_all x1, waiting for transfers between devices, local(): second = lax.all_to_all(codes, 'depth', 0, 0, tiled=True)  15.1 us
    ppermute x4, starting transfers between devices, turned(): lax.ppermute(value, axis, [(i, (i + by) % size) for i in range(size)])  8.59 us
    all_to_all x1, starting transfers between devices, local(): second = lax.all_to_all(codes, 'depth', 0, 0, tiled=True)  7.22 us
    all_to_all x1, starting transfers between devices, local(): first = lax.all_to_all(codes, 'depth', 0, 0, tiled=True)  4.07 us
    ppermute x4, waiting for transfers between devices, turned(): lax.ppermute(value, axis, [(i, (i + by) % size) for i in range(size)])  2.44 us
    pallas_call x2, Pallas kernels, merge(): pl.pallas_call(kernel, in_specs=[pl.BlockSpec(memory_space=pltpu.VMEM), w...  2.25 us
  transfers between devices with their start and end apart: 6, of which 2 were waited for; matrix products, arithmetic and copies ran while one was open for 2% of the time, Pallas kernels for 34%

profile of v4, /device:TPU:0, one launch (start us, length us, event | category | flops | bytes accessed | tf_op | source)
XLA Modules:
  0.0 81.5 jit_solution(5744310715176648550)
XLA Ops:
  0.0 1.3 %slice_bitcast_fusion = (bf16[128,2048]{1,0:T(8,128)(2,1)S(1)}, bf16[128,2048]{1,0:T(8,128)(2,1)S(1)}) fusion(bf16[16,128,2048]{2,1,0:T(8,128)(2,1)} %refs_1_.5), kind=kLoop, calls=%fused_computation | loop fusion | bytes 2097152 | tf_op jit(solution)/shard_map/squeeze | solution.py:428
  1.3 5.4 %collective-permute-start.1 = (bf16[128,2048]{1,0:T(8,128)(2,1)S(1)}, bf16[128,2048]{1,0:T(8,128)(2,1)S(1)}, u32[]{:S(2)}, u32[]{:S(2)}) collective-permute-start(bf16[128,2048]{1,0:T(8,128)(2,1)S(1)} %get-tuple-element.11), channel_id=1, source_target_pairs={{0,120},{8,0},{16,8},{24,16},{32,24},{40,32},{48,40},{56,48},{64,5... | collective-permute-start | bytes 1572872 | tf_op jit(solution)/shard_map/ppermute | solution.py:425
  6.7 0.0 collective-permute-start
  6.7 1.4 %fusion = (bf16[16,1,2048]{2,1,0:T(2,128)(2,1)S(1)}, bf16[16,1,2048]{2,1,0:T(2,128)(2,1)S(1)}) fusion(bf16[16,128,2048]{2,1,0:T(8,128)(2,1)} %refs_1_.5), kind=kLoop, calls=%fused_computation.4 | loop fusion | bytes 262144 | tf_op jit(solution)/shard_map/slice | solution.py:430
  8.1 0.0 collective-permute-start.2
  8.2 3.2 %collective-permute-start.3 = (bf16[16,2048]{1,0:T(8,128)(2,1)S(1)}, bf16[16,2048]{1,0:T(8,128)(2,1)S(1)}, u32[]{:S(2)}, u32[]{:S(2)}) collective-permute-start(bf16[16,2048]{1,0:T(8,128)(2,1)S(1)} %bitcast.11), channel_id=1, source_target_pairs={{0,7},{1,0},{2,1},{3,2},{4,3},{5,4},{6,5},{7,6},{8,15},{9,8},{10,9... | collective-permute-start | bytes 196616 | tf_op jit(solution)/shard_map/ppermute | solution.py:425
  11.4 9.5 %mid_layers.1.refs_7_ = f32[16,4,32,128]{3,2,1,0:T(8,128)S(1)} custom-call(f32[4,16]{1,0:T(4,128)} %refs_0_.5, bf16[16,128,2048]{2,1,0:T(8,128)(2,1)} %refs_1_.5, s32[16,128,2048]{2,1,0:T(8,128)} %refs_2_.5), custom_call_target="tpu_custom_call" | custom-call | tf_op jit(solution)/shard_map/mid_layers/pallas_call | solution.py:359
  20.9 0.0 collective-permute-done.2.refs_5_
  20.9 0.0 collective-permute-done.3.refs_6_
  20.9 0.0 collective-permute-done.1.refs_4_
  20.9 2.4 %collective-permute-done.refs_3_ = bf16[128,2048]{1,0:T(8,128)(2,1)S(1)} collective-permute-done((bf16[128,2048]{1,0:T(8,128)(2,1)S(1)}, bf16[128,2048]{1,0:T(8,128)(2,1)S(1)}, u32[]{:S(2)}, u32[]{:S(2)}) %collective-permute-start) | collective-permute-done | bytes 524320 | tf_op jit(solution)/shard_map/ppermute | solution.py:425
  23.4 12.7 %ends_all_layers.1 = s16[16,4,64,128]{3,2,1,0:T(8,128)(2,1)} custom-call(f32[4,16]{1,0:T(4,128)} %refs_0_.5, bf16[16,128,2048]{2,1,0:T(8,128)(2,1)} %refs_1_.5, s32[16,128,2048]{2,1,0:T(8,128)} %refs_2_.5, bf16[128,2048]{1,0:T(8,128)(2,1)S(1)} %collective-permute-done.refs_3_, bf16[128,2048]{1,0:T(8,128)(2,1)S(1)} %collective-permute-done.1.refs_4_, ...), custom_call_target="tpu_custom_call" | custom-call | tf_op jit(solution)/shard_map/ends_all_layers/pallas_call | solution.py:359
  36.1 4.1 %all-to-all-start.1 = ((s16[16,4,64,128]{3,2,1,0:T(8,128)(2,1)}), s16[16,4,64,128]{3,2,1,0:T(8,128)(2,1)S(1)}, u32[]{:S(2)}, u32[]{:S(2)}) async-start(s16[16,4,64,128]{3,2,1,0:T(8,128)(2,1)} %ends_all_layers.1), calls=%async_computation.1 | async-start | bytes 2097152 | tf_op jit(solution)/shard_map/all_to_all | solution.py:439
  40.2 16.7 %all_layers.1 = s16[16,4,64,128]{3,2,1,0:T(8,128)(2,1)} custom-call(f32[4,16]{1,0:T(4,128)} %refs_0_.5, bf16[16,128,2048]{2,1,0:T(8,128)(2,1)} %refs_1_.5, s32[16,128,2048]{2,1,0:T(8,128)} %refs_2_.5, bf16[128,2048]{1,0:T(8,128)(2,1)S(1)} %collective-permute-done.refs_3_, bf16[128,2048]{1,0:T(8,128)(2,1)S(1)} %collective-permute-done.1.refs_4_, ...), custom_call_target="tpu_custom_call" | custom-call | tf_op jit(solution)/shard_map/all_layers/pallas_call | solution.py:359
  56.9 0.0 all-to-all-done.1.refs_0_
  56.9 7.2 %all-to-all-start = ((s16[16,4,64,128]{3,2,1,0:T(8,128)(2,1)}), s16[16,4,64,128]{3,2,1,0:T(8,128)(2,1)S(1)}, u32[]{:S(2)}, u32[]{:S(2)}) async-start(s16[16,4,64,128]{3,2,1,0:T(8,128)(2,1)} %all_layers.1), calls=%async_computation | async-start | bytes 2097152 | tf_op jit(solution)/shard_map/all_to_all | solution.py:441
  64.2 1.1 %merge.2.refs_1_ = f32[4,128,128]{2,1,0:T(8,128)} custom-call(s16[16,4,64,128]{3,2,1,0:T(8,128)(2,1)S(1)} %all-to-all-done.1.refs_0_), custom_call_target="tpu_custom_call" | custom-call | tf_op jit(solution)/shard_map/merge/pallas_call | solution.py:402
  65.3 15.1 %all-to-all-done.refs_0_ = s16[16,4,64,128]{3,2,1,0:T(8,128)(2,1)S(1)} async-done(((s16[16,4,64,128]{3,2,1,0:T(8,128)(2,1)}), s16[16,4,64,128]{3,2,1,0:T(8,128)(2,1)S(1)}, u32[]{:S(2)}, u32[]{:S(2)}) %all-to-all-start) | async-done | bytes 1048608 | tf_op jit(solution)/shard_map/all_to_all | solution.py:441
  80.4 1.1 %merge.3 = f32[4,128,128]{2,1,0:T(8,128)} custom-call(s16[16,4,64,128]{3,2,1,0:T(8,128)(2,1)S(1)} %all-to-all-done.refs_0_, f32[4,128,128]{2,1,0:T(8,128)} %merge.2.refs_1_), custom_call_target="tpu_custom_call", output_to_operand_aliasing={{}: (1, {})} | custom-call | tf_op jit(solution)/shard_map/merge/pallas_call | solution.py:402
  (2 shorter events, 0.1 us)
Async XLA Ops:
  1.3 19.6 %collective-permute-start.1 = (bf16[128,2048]{1,0:T(8,128)(2,1)S(1)}, bf16[128,2048]{1,0:T(8,128)(2,1)S(1)}, u32[]{:S(2)}, u32[]{:S(2)}) collective-permute-start(bf16[128,2048]{1,0:T(8,128)(2,1)S(1)} %get-tuple-element.11), channel_id=1, source_target_pairs={{0,120},{8,0},{16,8},{24,16},{32,24},{40,32},{48,40},{56,48},{64,5... | collective-permute-start | bytes 1572872 | tf_op jit(solution)/shard_map/ppermute | solution.py:425
  6.7 16.7 %collective-permute-start = (bf16[128,2048]{1,0:T(8,128)(2,1)S(1)}, bf16[128,2048]{1,0:T(8,128)(2,1)S(1)}, u32[]{:S(2)}, u32[]{:S(2)}) collective-permute-start(bf16[128,2048]{1,0:T(8,128)(2,1)S(1)} %get-tuple-element.12), channel_id=1, source_target_pairs={{0,8},{8,16},{16,24},{24,32},{32,40},{40,48},{48,56},{56,64},{64,7... | collective-permute-start | bytes 1572872 | tf_op jit(solution)/shard_map/ppermute | solution.py:425
  8.1 12.8 %collective-permute-start.2 = (bf16[16,2048]{1,0:T(8,128)(2,1)S(1)}, bf16[16,2048]{1,0:T(8,128)(2,1)S(1)}, u32[]{:S(2)}, u32[]{:S(2)}) collective-permute-start(bf16[16,2048]{1,0:T(8,128)(2,1)S(1)} %bitcast.10), channel_id=1, source_target_pairs={{0,1},{1,2},{2,3},{3,4},{4,5},{5,6},{6,7},{7,0},{8,9},{9,10},{10,1... | collective-permute-start | bytes 196616 | tf_op jit(solution)/shard_map/ppermute | solution.py:425
  8.2 12.7 %collective-permute-start.3 = (bf16[16,2048]{1,0:T(8,128)(2,1)S(1)}, bf16[16,2048]{1,0:T(8,128)(2,1)S(1)}, u32[]{:S(2)}, u32[]{:S(2)}) collective-permute-start(bf16[16,2048]{1,0:T(8,128)(2,1)S(1)} %bitcast.11), channel_id=1, source_target_pairs={{0,7},{1,0},{2,1},{3,2},{4,3},{5,4},{6,5},{7,6},{8,15},{9,8},{10,9... | collective-permute-start | bytes 196616 | tf_op jit(solution)/shard_map/ppermute | solution.py:425
  36.1 20.8 %all-to-all-start.1 = ((s16[16,4,64,128]{3,2,1,0:T(8,128)(2,1)}), s16[16,4,64,128]{3,2,1,0:T(8,128)(2,1)S(1)}, u32[]{:S(2)}, u32[]{:S(2)}) async-start(s16[16,4,64,128]{3,2,1,0:T(8,128)(2,1)} %ends_all_layers.1), calls=%async_computation.1 | async-start | bytes 2097152 | tf_op jit(solution)/shard_map/all_to_all | solution.py:439
  56.9 23.5 %all-to-all-start = ((s16[16,4,64,128]{3,2,1,0:T(8,128)(2,1)}), s16[16,4,64,128]{3,2,1,0:T(8,128)(2,1)S(1)}, u32[]{:S(2)}, u32[]{:S(2)}) async-start(s16[16,4,64,128]{3,2,1,0:T(8,128)(2,1)} %all_layers.1), calls=%async_computation | async-start | bytes 2097152 | tf_op jit(solution)/shard_map/all_to_all | solution.py:441

commit v5 on v4

--- a/solution.py
+++ b/solution.py
@@ -44,7 +44,7 @@
     while share % batch or (stride > 1 and batch > 1):
         batch -= 1
 
-    load = columns if mode == "ends" else LOAD
+    load = 2 * LOAD if mode == "ends" else LOAD
     loads, each = columns // load, load // PIECE
     ahead = 2 if each == 1 else 1
     adjacent = segments[1][0] == segments[0][0] + height
@@ -251,16 +251,18 @@
             both((i, 0, first_set), (i, 1, second_set))
             both((i, 1, second_set), (jnp.minimum(i + 1, count - 1), 0, first_set))
 
-            @pl.when(i % each == each - 1)
-            def _():
-                out_copy(i // each).start()
+            if out_hbm is not None:
+
+                @pl.when(i % each == each - 1)
+                def _():
+                    out_copy(i // each).start()
 
             return carry
 
         lax.fori_loop(0, count, body, 0)
 
     def finish():
-        for p in range(loads):
+        for p in range(loads if out_hbm is not None else 0):
             out_copy(p).wait()
 
     return begin, run, finish
@@ -284,7 +286,8 @@
     blocks = columns // LANES
     rows_of = [2 * segments[0][1] for segments, mode in groups]
     total = sum(rows_of)
-    out_type = f32 if groups[0][1] == "mid" else jnp.int16
+    direct = groups[0][1] == "mid"
+    out_type = f32 if direct else jnp.int16
     whole = pl.BlockSpec(memory_space=pltpu.HBM)
     inside = pl.BlockSpec(memory_space=pltpu.VMEM)
     given = {"table": (table, whole), "heat": (heat, whole), "entry": (entry, whole)}
@@ -293,16 +296,14 @@
     if upper is not None:
         given["upper"], given["lower"] = (upper, inside), (lower, inside)
     if state is not None:
-        given["state"] = (state, whole)
+        given["state"] = (state, inside)
     names = list(given)
     common = [
         pltpu.VMEM(table.shape, f32),
         pltpu.VMEM((SUBLANES, LANES), f32),
         pltpu.VMEM((2, layers, columns), f32),
         pltpu.VMEM((PIECE + 2 * LANES, PIECE), jnp.bfloat16),
-        pltpu.VMEM((blocks, 4, total, LANES), out_type),
-        pltpu.VMEM((blocks, 4, 2 * groups[0][0][0][1] if state is not None else SUBLANES, LANES), f32),
-        pltpu.SemaphoreType.DMA,
+        pltpu.VMEM((SUBLANES, LANES) if direct else (blocks, 4, total, LANES), out_type),
         pltpu.SemaphoreType.DMA,
     ]
     own = []
@@ -324,19 +325,18 @@
     def kernel(*refs):
         ref = dict(zip(names, refs))
         out_hbm = refs[len(names)]
-        table_ref, padded, rim_rows, weights, out_ref, state_ref, state_sem, table_sem, *rest = refs[len(names) + 1 :]
+        table_ref, padded, rim_rows, weights, out_ref, table_sem, *rest = refs[len(names) + 1 :]
+        if direct:
+            out_hbm, out_ref = None, out_hbm
         here, side = lax.axis_index("depth"), lax.axis_index("cross")
         flags = [(here > 0).astype(f32), (here < lax.axis_size("depth") - 1).astype(f32)]
         table_copy = pltpu.make_async_copy(ref["table"], table_ref, table_sem)
         table_copy.start()
         tables = []
-        if state is not None:
-            state_copy = pltpu.make_async_copy(ref["state"], state_ref, state_sem)
-            state_copy.start()
         runs, row = [], 0
         for n, (segments, mode) in enumerate(groups):
             runs.append(
-                strip_pipeline(tables, rim_rows, flags, ref.get("before"), ref.get("after"), ref["heat"], ref["entry"], state_ref,
+                strip_pipeline(tables, rim_rows, flags, ref.get("before"), ref.get("after"), ref["heat"], ref["entry"], ref.get("state"),
                                out_hbm, out_ref, row, weights, *rest[8 * n : 8 * n + 8], segments=segments, mode=mode, sight=sight)
             )
             row += rows_of[n]
@@ -349,8 +349,6 @@
         weights[...] = jnp.where(k == LANES + 1, 1.0, jnp.where(k == LANES - 1, -1.0, 0.0)).astype(jnp.bfloat16)
         table_copy.wait()
         tables += lookup_words(table_ref, padded)
-        if state is not None:
-            state_copy.wait()
         for begin, run, finish in runs:
             run()
         for begin, run, finish in runs:
@@ -359,7 +357,7 @@
     return pl.pallas_call(
         kernel,
         in_specs=[given[name][1] for name in names],
-        out_specs=whole,
+        out_specs=inside if direct else whole,
         out_shape=jax.ShapeDtypeStruct((blocks, 4, total, LANES), out_type),
         scratch_shapes=common + own,
         compiler_params=pltpu.CompilerParams(vmem_limit_bytes=36 * 1024 * 1024),
@@ -432,14 +430,14 @@
     heat = pltpu.with_memory_space_constraint(heat, pltpu.HBM)
     entry = pltpu.with_memory_space_constraint(entry, pltpu.HBM)
     table = pltpu.with_memory_space_constraint(table, pltpu.HBM)
-    centre, inner, outer = ((48, 16), (64, 16)), ((32, 16), (80, 16)), ((0, 32), (96, 32))
+    centre, outer = ((32, 32), (64, 32)), ((0, 32), (96, 32))
     state = brick(table, heat, entry, [(centre, "mid")], sight)
-    codes = brick(table, heat, entry, [(centre, "ends"), (inner, "all")], sight, before=before, after=after, upper=upper, lower=lower, state=state)
+    codes = brick(table, heat, entry, [(centre, "ends")], sight, before=before, after=after, upper=upper, lower=lower, state=state)
     codes, before = lax.optimization_barrier((codes, before))
     first = lax.all_to_all(codes, "depth", 0, 0, tiled=True)
     codes = brick(table, heat, entry, [(outer, "all")], sight, before=before, after=after, upper=upper, lower=lower)
     second = lax.all_to_all(codes, "depth", 0, 0, tiled=True)
-    image = merge(first, None, rows, (3, 4, 2, 5))
+    image = merge(first, None, rows, (2, 3, 4, 5))
     return merge(second, image, rows, (0, 1, 6, 7))
 
 

time: 81.9 us -> 79.7 us (0.973)
  waiting for transfers between devices: 17.6 us -> 15.1 us
  starting transfers between devices: 19.9 us -> 22.3 us
  Pallas kernels: 41.2 us -> 39 us
    ppermute x4, waiting for transfers between devices: 2.44 us -> 0.01 us  [turned(): lax.ppermute(value, axis, [(i, (i + by) % size) for i in range(size)])]
    all_to_all x1, starting transfers between devices: 4.07 us -> 6.47 us  [local(): first = lax.all_to_all(codes, 'depth', 0, 0, tiled=True)]
    pallas_call x3, Pallas kernels: 38.9 us -> 36.8 us  [brick(): pl.pallas_call(kernel, in_specs=[given[name][1] for name in names], out_s...]
  transfers between devices with their start and end apart: 6 -> 6, of which waited for: 2 -> 1; matrix products, arithmetic and copies ran while one was open for 2% -> 2% of each run, Pallas kernels for 34% -> 41%
where the time goes in v5:
time: 79.7 us; the launch traced here: 79.4 us
  Pallas kernels  39 us (49%)
  starting transfers between devices  22.3 us (28%)
  waiting for transfers between devices  15.1 us (19%)
  local copies, waits for them, and re-layouts  2.79 us (4%)
    pallas_call x3, Pallas kernels, brick(): pl.pallas_call(kernel, in_specs=[given[name][1] for name in names], out_s...  36.8 us
    all_to_all x1, waiting for transfers between devices, local(): second = lax.all_to_all(codes, 'depth', 0, 0, tiled=True)  15.1 us
    ppermute x4, starting transfers between devices, turned(): lax.ppermute(value, axis, [(i, (i + by) % size) for i in range(size)])  8.59 us
    all_to_all x1, starting transfers between devices, local(): second = lax.all_to_all(codes, 'depth', 0, 0, tiled=True)  7.22 us
    all_to_all x1, starting transfers between devices, local(): first = lax.all_to_all(codes, 'depth', 0, 0, tiled=True)  6.47 us
    pallas_call x2, Pallas kernels, merge(): pl.pallas_call(kernel, in_specs=[pl.BlockSpec(memory_space=pltpu.VMEM), w...  2.25 us
  transfers between devices with their start and end apart: 6, of which 1 were waited for; matrix products, arithmetic and copies ran while one was open for 2% of the time, Pallas kernels for 41%

profile of v5, /device:TPU:0, one launch (start us, length us, event | category | flops | bytes accessed | tf_op | source)
XLA Modules:
  0.0 79.4 jit_solution(6311503246754741575)
XLA Ops:
  0.0 1.3 %slice_bitcast_fusion = (bf16[128,2048]{1,0:T(8,128)(2,1)S(1)}, bf16[128,2048]{1,0:T(8,128)(2,1)S(1)}) fusion(bf16[16,128,2048]{2,1,0:T(8,128)(2,1)} %refs_1_.5), kind=kLoop, calls=%fused_computation | loop fusion | bytes 2097152 | tf_op jit(solution)/shard_map/squeeze | solution.py:426
  1.3 5.4 %collective-permute-start.1 = (bf16[128,2048]{1,0:T(8,128)(2,1)S(1)}, bf16[128,2048]{1,0:T(8,128)(2,1)S(1)}, u32[]{:S(2)}, u32[]{:S(2)}) collective-permute-start(bf16[128,2048]{1,0:T(8,128)(2,1)S(1)} %get-tuple-element.11), channel_id=1, source_target_pairs={{0,120},{8,0},{16,8},{24,16},{32,24},{40,32},{48,40},{56,48},{64,5... | collective-permute-start | bytes 1572872 | tf_op jit(solution)/shard_map/ppermute | solution.py:423
  6.7 0.0 collective-permute-start
  6.7 1.4 %fusion = (bf16[16,1,2048]{2,1,0:T(2,128)(2,1)S(1)}, bf16[16,1,2048]{2,1,0:T(2,128)(2,1)S(1)}) fusion(bf16[16,128,2048]{2,1,0:T(8,128)(2,1)} %refs_1_.5), kind=kLoop, calls=%fused_computation.4 | loop fusion | bytes 262144 | tf_op jit(solution)/shard_map/slice | solution.py:428
  8.1 0.0 collective-permute-start.2
  8.2 3.2 %collective-permute-start.3 = (bf16[16,2048]{1,0:T(8,128)(2,1)S(1)}, bf16[16,2048]{1,0:T(8,128)(2,1)S(1)}, u32[]{:S(2)}, u32[]{:S(2)}) collective-permute-start(bf16[16,2048]{1,0:T(8,128)(2,1)S(1)} %bitcast.11), channel_id=1, source_target_pairs={{0,7},{1,0},{2,1},{3,2},{4,3},{5,4},{6,5},{7,6},{8,15},{9,8},{10,9... | collective-permute-start | bytes 196616 | tf_op jit(solution)/shard_map/ppermute | solution.py:423
  11.4 14.6 %mid_layers.1.refs_7_ = f32[16,4,64,128]{3,2,1,0:T(8,128)S(1)} custom-call(f32[4,16]{1,0:T(4,128)} %refs_0_.5, bf16[16,128,2048]{2,1,0:T(8,128)(2,1)} %refs_1_.5, s32[16,128,2048]{2,1,0:T(8,128)} %refs_2_.5), custom_call_target="tpu_custom_call" | custom-call | tf_op jit(solution)/shard_map/mid_layers/pallas_call | solution.py:357
  26.0 0.0 collective-permute-done.2.refs_5_
  26.1 0.0 collective-permute-done.3.refs_6_
  26.1 0.0 collective-permute-done.1.refs_4_
  26.1 0.0 collective-permute-done.refs_3_
  26.1 5.4 %ends_layers.1 = s16[16,4,64,128]{3,2,1,0:T(8,128)(2,1)} custom-call(f32[4,16]{1,0:T(4,128)} %refs_0_.5, bf16[16,128,2048]{2,1,0:T(8,128)(2,1)} %refs_1_.5, s32[16,128,2048]{2,1,0:T(8,128)} %refs_2_.5, bf16[128,2048]{1,0:T(8,128)(2,1)S(1)} %collective-permute-done.refs_3_, bf16[128,2048]{1,0:T(8,128)(2,1)S(1)} %collective-permute-done.1.refs_4_, ...), custom_call_target="tpu_custom_call" | custom-call | tf_op jit(solution)/shard_map/ends_layers/pallas_call | solution.py:357
  31.5 6.5 %all-to-all-start.1 = ((s16[16,4,64,128]{3,2,1,0:T(8,128)(2,1)}), s16[16,4,64,128]{3,2,1,0:T(8,128)(2,1)S(1)}, u32[]{:S(2)}, u32[]{:S(2)}) async-start(s16[16,4,64,128]{3,2,1,0:T(8,128)(2,1)} %ends_layers.1), calls=%async_computation.1 | async-start | bytes 2097152 | tf_op jit(solution)/shard_map/all_to_all | solution.py:437
  38.0 16.7 %all_layers.1 = s16[16,4,64,128]{3,2,1,0:T(8,128)(2,1)} custom-call(f32[4,16]{1,0:T(4,128)} %refs_0_.5, bf16[16,128,2048]{2,1,0:T(8,128)(2,1)} %refs_1_.5, s32[16,128,2048]{2,1,0:T(8,128)} %refs_2_.5, bf16[128,2048]{1,0:T(8,128)(2,1)S(1)} %collective-permute-done.refs_3_, bf16[128,2048]{1,0:T(8,128)(2,1)S(1)} %collective-permute-done.1.refs_4_, ...), custom_call_target="tpu_custom_call" | custom-call | tf_op jit(solution)/shard_map/all_layers/pallas_call | solution.py:357
  54.7 0.0 all-to-all-done.1.refs_0_
  54.8 7.2 %all-to-all-start = ((s16[16,4,64,128]{3,2,1,0:T(8,128)(2,1)}), s16[16,4,64,128]{3,2,1,0:T(8,128)(2,1)S(1)}, u32[]{:S(2)}, u32[]{:S(2)}) async-start(s16[16,4,64,128]{3,2,1,0:T(8,128)(2,1)} %all_layers.1), calls=%async_computation | async-start | bytes 2097152 | tf_op jit(solution)/shard_map/all_to_all | solution.py:439
  62.0 1.1 %merge.2.refs_1_ = f32[4,128,128]{2,1,0:T(8,128)} custom-call(s16[16,4,64,128]{3,2,1,0:T(8,128)(2,1)S(1)} %all-to-all-done.1.refs_0_), custom_call_target="tpu_custom_call" | custom-call | tf_op jit(solution)/shard_map/merge/pallas_call | solution.py:400
  63.1 15.1 %all-to-all-done.refs_0_ = s16[16,4,64,128]{3,2,1,0:T(8,128)(2,1)S(1)} async-done(((s16[16,4,64,128]{3,2,1,0:T(8,128)(2,1)}), s16[16,4,64,128]{3,2,1,0:T(8,128)(2,1)S(1)}, u32[]{:S(2)}, u32[]{:S(2)}) %all-to-all-start) | async-done | bytes 1048608 | tf_op jit(solution)/shard_map/all_to_all | solution.py:439
  78.2 1.1 %merge.3 = f32[4,128,128]{2,1,0:T(8,128)} custom-call(s16[16,4,64,128]{3,2,1,0:T(8,128)(2,1)S(1)} %all-to-all-done.refs_0_, f32[4,128,128]{2,1,0:T(8,128)} %merge.2.refs_1_), custom_call_target="tpu_custom_call", output_to_operand_aliasing={{}: (1, {})} | custom-call | tf_op jit(solution)/shard_map/merge/pallas_call | solution.py:400
  (2 shorter events, 0.1 us)
Async XLA Ops:
  1.3 24.8 %collective-permute-start.1 = (bf16[128,2048]{1,0:T(8,128)(2,1)S(1)}, bf16[128,2048]{1,0:T(8,128)(2,1)S(1)}, u32[]{:S(2)}, u32[]{:S(2)}) collective-permute-start(bf16[128,2048]{1,0:T(8,128)(2,1)S(1)} %get-tuple-element.11), channel_id=1, source_target_pairs={{0,120},{8,0},{16,8},{24,16},{32,24},{40,32},{48,40},{56,48},{64,5... | collective-permute-start | bytes 1572872 | tf_op jit(solution)/shard_map/ppermute | solution.py:423
  6.7 19.4 %collective-permute-start = (bf16[128,2048]{1,0:T(8,128)(2,1)S(1)}, bf16[128,2048]{1,0:T(8,128)(2,1)S(1)}, u32[]{:S(2)}, u32[]{:S(2)}) collective-permute-start(bf16[128,2048]{1,0:T(8,128)(2,1)S(1)} %get-tuple-element.12), channel_id=1, source_target_pairs={{0,8},{8,16},{16,24},{24,32},{32,40},{40,48},{48,56},{56,64},{64,7... | collective-permute-start | bytes 1572872 | tf_op jit(solution)/shard_map/ppermute | solution.py:423
  8.1 17.9 %collective-permute-start.2 = (bf16[16,2048]{1,0:T(8,128)(2,1)S(1)}, bf16[16,2048]{1,0:T(8,128)(2,1)S(1)}, u32[]{:S(2)}, u32[]{:S(2)}) collective-permute-start(bf16[16,2048]{1,0:T(8,128)(2,1)S(1)} %bitcast.10), channel_id=1, source_target_pairs={{0,1},{1,2},{2,3},{3,4},{4,5},{5,6},{6,7},{7,0},{8,9},{9,10},{10,1... | collective-permute-start | bytes 196616 | tf_op jit(solution)/shard_map/ppermute | solution.py:423
  8.2 17.8 %collective-permute-start.3 = (bf16[16,2048]{1,0:T(8,128)(2,1)S(1)}, bf16[16,2048]{1,0:T(8,128)(2,1)S(1)}, u32[]{:S(2)}, u32[]{:S(2)}) collective-permute-start(bf16[16,2048]{1,0:T(8,128)(2,1)S(1)} %bitcast.11), channel_id=1, source_target_pairs={{0,7},{1,0},{2,1},{3,2},{4,3},{5,4},{6,5},{7,6},{8,15},{9,8},{10,9... | collective-permute-start | bytes 196616 | tf_op jit(solution)/shard_map/ppermute | solution.py:423
  31.5 23.2 %all-to-all-start.1 = ((s16[16,4,64,128]{3,2,1,0:T(8,128)(2,1)}), s16[16,4,64,128]{3,2,1,0:T(8,128)(2,1)S(1)}, u32[]{:S(2)}, u32[]{:S(2)}) async-start(s16[16,4,64,128]{3,2,1,0:T(8,128)(2,1)} %ends_layers.1), calls=%async_computation.1 | async-start | bytes 2097152 | tf_op jit(solution)/shard_map/all_to_all | solution.py:437
  54.8 23.5 %all-to-all-start = ((s16[16,4,64,128]{3,2,1,0:T(8,128)(2,1)}), s16[16,4,64,128]{3,2,1,0:T(8,128)(2,1)S(1)}, u32[]{:S(2)}, u32[]{:S(2)}) async-start(s16[16,4,64,128]{3,2,1,0:T(8,128)(2,1)} %all_layers.1), calls=%async_computation | async-start | bytes 2097152 | tf_op jit(solution)/shard_map/all_to_all | solution.py:439

commit v6 on v5

--- a/solution.py
+++ b/solution.py
@@ -44,7 +44,7 @@
     while share % batch or (stride > 1 and batch > 1):
         batch -= 1
 
-    load = 2 * LOAD if mode == "ends" else LOAD
+    load = LOAD
     loads, each = columns // load, load // PIECE
     ahead = 2 if each == 1 else 1
     adjacent = segments[1][0] == segments[0][0] + height
@@ -106,8 +106,9 @@
             start(entry_copies(p))
             if p + ahead < loads:
                 start(heat_copies(p + ahead))
-        heat[:, :, :, 0 : 2 * LANES] = jnp.zeros(heat.shape[:3] + (2 * LANES,), jnp.bfloat16)
-        heat[:, :, :, 2 * LANES + columns :] = jnp.zeros(heat.shape[:3] + (LANES,), jnp.bfloat16)
+        margin = jnp.zeros(heat.shape[:2] + (height, LANES), jnp.bfloat16)
+        heat[:, :, 16 : 16 + height, LANES : 2 * LANES] = margin
+        heat[:, :, 16 : 16 + height, 2 * LANES + columns :] = margin
         k = lax.broadcasted_iota(jnp.int32, rows_by.shape, 1) - lax.broadcasted_iota(jnp.int32, rows_by.shape, 0)
         rows_by[...] = jnp.where(k == 17, 1.0, jnp.where(k == 15, -1.0, 0.0)).astype(jnp.bfloat16)
         across = slice(2 * LANES, 2 * LANES + columns)

time: 79.7 us -> 79.5 us (level)
  no operation moved by 1% of the time
where the time goes in v6:
time: 79.5 us; the launch traced here: 79.2 us
  Pallas kernels  38.9 us (49%)
  starting transfers between devices  22.3 us (28%)
  waiting for transfers between devices  15.1 us (19%)
  local copies, waits for them, and re-layouts  2.79 us (4%)
    pallas_call x3, Pallas kernels, brick(): pl.pallas_call(kernel, in_specs=[given[name][1] for name in names], out_s...  36.6 us
    all_to_all x1, waiting for transfers between devices, local(): second = lax.all_to_all(codes, 'depth', 0, 0, tiled=True)  15.1 us
    ppermute x4, starting transfers between devices, turned(): lax.ppermute(value, axis, [(i, (i + by) % size) for i in range(size)])  8.59 us
    all_to_all x1, starting transfers between devices, local(): second = lax.all_to_all(codes, 'depth', 0, 0, tiled=True)  7.22 us
    all_to_all x1, starting transfers between devices, local(): first = lax.all_to_all(codes, 'depth', 0, 0, tiled=True)  6.47 us
    pallas_call x2, Pallas kernels, merge(): pl.pallas_call(kernel, in_specs=[pl.BlockSpec(memory_space=pltpu.VMEM), w...  2.25 us
  transfers between devices with their start and end apart: 6, of which 1 were waited for; matrix products, arithmetic and copies ran while one was open for 2% of the time, Pallas kernels for 41%

profile of v6, /device:TPU:0, one launch (start us, length us, event | category | flops | bytes accessed | tf_op | source)
XLA Modules:
  0.0 79.2 jit_solution(16164531714165059167)
XLA Ops:
  0.0 1.3 %slice_bitcast_fusion = (bf16[128,2048]{1,0:T(8,128)(2,1)S(1)}, bf16[128,2048]{1,0:T(8,128)(2,1)S(1)}) fusion(bf16[16,128,2048]{2,1,0:T(8,128)(2,1)} %refs_1_.5), kind=kLoop, calls=%fused_computation | loop fusion | bytes 2097152 | tf_op jit(solution)/shard_map/squeeze | solution.py:427
  1.3 5.4 %collective-permute-start.1 = (bf16[128,2048]{1,0:T(8,128)(2,1)S(1)}, bf16[128,2048]{1,0:T(8,128)(2,1)S(1)}, u32[]{:S(2)}, u32[]{:S(2)}) collective-permute-start(bf16[128,2048]{1,0:T(8,128)(2,1)S(1)} %get-tuple-element.11), channel_id=1, source_target_pairs={{0,120},{8,0},{16,8},{24,16},{32,24},{40,32},{48,40},{56,48},{64,5... | collective-permute-start | bytes 1572872 | tf_op jit(solution)/shard_map/ppermute | solution.py:424
  6.7 0.0 collective-permute-start
  6.7 1.4 %fusion = (bf16[16,1,2048]{2,1,0:T(2,128)(2,1)S(1)}, bf16[16,1,2048]{2,1,0:T(2,128)(2,1)S(1)}) fusion(bf16[16,128,2048]{2,1,0:T(8,128)(2,1)} %refs_1_.5), kind=kLoop, calls=%fused_computation.4 | loop fusion | bytes 262144 | tf_op jit(solution)/shard_map/slice | solution.py:429
  8.1 0.0 collective-permute-start.2
  8.2 3.2 %collective-permute-start.3 = (bf16[16,2048]{1,0:T(8,128)(2,1)S(1)}, bf16[16,2048]{1,0:T(8,128)(2,1)S(1)}, u32[]{:S(2)}, u32[]{:S(2)}) collective-permute-start(bf16[16,2048]{1,0:T(8,128)(2,1)S(1)} %bitcast.11), channel_id=1, source_target_pairs={{0,7},{1,0},{2,1},{3,2},{4,3},{5,4},{6,5},{7,6},{8,15},{9,8},{10,9... | collective-permute-start | bytes 196616 | tf_op jit(solution)/shard_map/ppermute | solution.py:424
  11.4 14.6 %mid_layers.1.refs_7_ = f32[16,4,64,128]{3,2,1,0:T(8,128)S(1)} custom-call(f32[4,16]{1,0:T(4,128)} %refs_0_.5, bf16[16,128,2048]{2,1,0:T(8,128)(2,1)} %refs_1_.5, s32[16,128,2048]{2,1,0:T(8,128)} %refs_2_.5), custom_call_target="tpu_custom_call" | custom-call | tf_op jit(solution)/shard_map/mid_layers/pallas_call | solution.py:358
  26.0 0.0 collective-permute-done.2.refs_5_
  26.1 0.0 collective-permute-done.3.refs_6_
  26.1 0.0 collective-permute-done.1.refs_4_
  26.1 0.0 collective-permute-done.refs_3_
  26.1 5.3 %ends_layers.1 = s16[16,4,64,128]{3,2,1,0:T(8,128)(2,1)} custom-call(f32[4,16]{1,0:T(4,128)} %refs_0_.5, bf16[16,128,2048]{2,1,0:T(8,128)(2,1)} %refs_1_.5, s32[16,128,2048]{2,1,0:T(8,128)} %refs_2_.5, bf16[128,2048]{1,0:T(8,128)(2,1)S(1)} %collective-permute-done.refs_3_, bf16[128,2048]{1,0:T(8,128)(2,1)S(1)} %collective-permute-done.1.refs_4_, ...), custom_call_target="tpu_custom_call" | custom-call | tf_op jit(solution)/shard_map/ends_layers/pallas_call | solution.py:358
  31.4 6.5 %all-to-all-start.1 = ((s16[16,4,64,128]{3,2,1,0:T(8,128)(2,1)}), s16[16,4,64,128]{3,2,1,0:T(8,128)(2,1)S(1)}, u32[]{:S(2)}, u32[]{:S(2)}) async-start(s16[16,4,64,128]{3,2,1,0:T(8,128)(2,1)} %ends_layers.1), calls=%async_computation.1 | async-start | bytes 2097152 | tf_op jit(solution)/shard_map/all_to_all | solution.py:438
  37.8 16.7 %all_layers.1 = s16[16,4,64,128]{3,2,1,0:T(8,128)(2,1)} custom-call(f32[4,16]{1,0:T(4,128)} %refs_0_.5, bf16[16,128,2048]{2,1,0:T(8,128)(2,1)} %refs_1_.5, s32[16,128,2048]{2,1,0:T(8,128)} %refs_2_.5, bf16[128,2048]{1,0:T(8,128)(2,1)S(1)} %collective-permute-done.refs_3_, bf16[128,2048]{1,0:T(8,128)(2,1)S(1)} %collective-permute-done.1.refs_4_, ...), custom_call_target="tpu_custom_call" | custom-call | tf_op jit(solution)/shard_map/all_layers/pallas_call | solution.py:358
  54.6 0.0 all-to-all-done.1.refs_0_
  54.6 7.2 %all-to-all-start = ((s16[16,4,64,128]{3,2,1,0:T(8,128)(2,1)}), s16[16,4,64,128]{3,2,1,0:T(8,128)(2,1)S(1)}, u32[]{:S(2)}, u32[]{:S(2)}) async-start(s16[16,4,64,128]{3,2,1,0:T(8,128)(2,1)} %all_layers.1), calls=%async_computation | async-start | bytes 2097152 | tf_op jit(solution)/shard_map/all_to_all | solution.py:440
  61.8 1.1 %merge.2.refs_1_ = f32[4,128,128]{2,1,0:T(8,128)} custom-call(s16[16,4,64,128]{3,2,1,0:T(8,128)(2,1)S(1)} %all-to-all-done.1.refs_0_), custom_call_target="tpu_custom_call" | custom-call | tf_op jit(solution)/shard_map/merge/pallas_call | solution.py:401
  63.0 15.1 %all-to-all-done.refs_0_ = s16[16,4,64,128]{3,2,1,0:T(8,128)(2,1)S(1)} async-done(((s16[16,4,64,128]{3,2,1,0:T(8,128)(2,1)}), s16[16,4,64,128]{3,2,1,0:T(8,128)(2,1)S(1)}, u32[]{:S(2)}, u32[]{:S(2)}) %all-to-all-start) | async-done | bytes 1048608 | tf_op jit(solution)/shard_map/all_to_all | solution.py:440
  78.1 1.1 %merge.3 = f32[4,128,128]{2,1,0:T(8,128)} custom-call(s16[16,4,64,128]{3,2,1,0:T(8,128)(2,1)S(1)} %all-to-all-done.refs_0_, f32[4,128,128]{2,1,0:T(8,128)} %merge.2.refs_1_), custom_call_target="tpu_custom_call", output_to_operand_aliasing={{}: (1, {})} | custom-call | tf_op jit(solution)/shard_map/merge/pallas_call | solution.py:401
  (2 shorter events, 0.1 us)
Async XLA Ops:
  1.3 24.8 %collective-permute-start.1 = (bf16[128,2048]{1,0:T(8,128)(2,1)S(1)}, bf16[128,2048]{1,0:T(8,128)(2,1)S(1)}, u32[]{:S(2)}, u32[]{:S(2)}) collective-permute-start(bf16[128,2048]{1,0:T(8,128)(2,1)S(1)} %get-tuple-element.11), channel_id=1, source_target_pairs={{0,120},{8,0},{16,8},{24,16},{32,24},{40,32},{48,40},{56,48},{64,5... | collective-permute-start | bytes 1572872 | tf_op jit(solution)/shard_map/ppermute | solution.py:424
  6.7 19.4 %collective-permute-start = (bf16[128,2048]{1,0:T(8,128)(2,1)S(1)}, bf16[128,2048]{1,0:T(8,128)(2,1)S(1)}, u32[]{:S(2)}, u32[]{:S(2)}) collective-permute-start(bf16[128,2048]{1,0:T(8,128)(2,1)S(1)} %get-tuple-element.12), channel_id=1, source_target_pairs={{0,8},{8,16},{16,24},{24,32},{32,40},{40,48},{48,56},{56,64},{64,7... | collective-permute-start | bytes 1572872 | tf_op jit(solution)/shard_map/ppermute | solution.py:424
  8.1 17.9 %collective-permute-start.2 = (bf16[16,2048]{1,0:T(8,128)(2,1)S(1)}, bf16[16,2048]{1,0:T(8,128)(2,1)S(1)}, u32[]{:S(2)}, u32[]{:S(2)}) collective-permute-start(bf16[16,2048]{1,0:T(8,128)(2,1)S(1)} %bitcast.10), channel_id=1, source_target_pairs={{0,1},{1,2},{2,3},{3,4},{4,5},{5,6},{6,7},{7,0},{8,9},{9,10},{10,1... | collective-permute-start | bytes 196616 | tf_op jit(solution)/shard_map/ppermute | solution.py:424
  8.2 17.8 %collective-permute-start.3 = (bf16[16,2048]{1,0:T(8,128)(2,1)S(1)}, bf16[16,2048]{1,0:T(8,128)(2,1)S(1)}, u32[]{:S(2)}, u32[]{:S(2)}) collective-permute-start(bf16[16,2048]{1,0:T(8,128)(2,1)S(1)} %bitcast.11), channel_id=1, source_target_pairs={{0,7},{1,0},{2,1},{3,2},{4,3},{5,4},{6,5},{7,6},{8,15},{9,8},{10,9... | collective-permute-start | bytes 196616 | tf_op jit(solution)/shard_map/ppermute | solution.py:424
  31.4 23.2 %all-to-all-start.1 = ((s16[16,4,64,128]{3,2,1,0:T(8,128)(2,1)}), s16[16,4,64,128]{3,2,1,0:T(8,128)(2,1)S(1)}, u32[]{:S(2)}, u32[]{:S(2)}) async-start(s16[16,4,64,128]{3,2,1,0:T(8,128)(2,1)} %ends_layers.1), calls=%async_computation.1 | async-start | bytes 2097152 | tf_op jit(solution)/shard_map/all_to_all | solution.py:438
  54.6 23.5 %all-to-all-start = ((s16[16,4,64,128]{3,2,1,0:T(8,128)(2,1)}), s16[16,4,64,128]{3,2,1,0:T(8,128)(2,1)S(1)}, u32[]{:S(2)}, u32[]{:S(2)}) async-start(s16[16,4,64,128]{3,2,1,0:T(8,128)(2,1)} %all_layers.1), calls=%async_computation | async-start | bytes 2097152 | tf_op jit(solution)/shard_map/all_to_all | solution.py:440
